TPU v7x, 128 devices: a whole 4x4x4 slice. The times are simulated.
128 devices in a mesh: clip: 8 (over y, core), sess: 16 (over z, x).
Axes of the slice: x: 4, y: 4, z: 4, core: 2. Of those that a mesh axis runs over, the one named last changes fastest.
Arguments:
- video: bfloat16 [128, 16, 2304], P('clip', 'sess'), may hold values from -6 to 6
- responses: bfloat16 [128, 16, 4096], P('clip', 'sess'), may hold values from 0 to 0.5
- assignment: int32 [128], P('clip'), may hold values from 0 to 15, as said below
- counts: int32 [16], P('sess'), may hold values from 1024 to 4096, as said below
- conv_weight: bfloat16 [64, 147], replicated, may hold values from -0.5 to 0.5
- conv_bias: float32 [64], replicated, may hold values from -3 to 3
- mix_weight: bfloat16 [64, 64], replicated, may hold values from -0.75 to 0.75
- mix_bias: float32 [64], replicated, may hold values from -3 to 3
- masks: bfloat16 [16, 4096, 576], P('sess'), may hold values from -0.25 to 0.25
- feat_w: bfloat16 [16, 4096, 64], P('sess'), may hold values from -0.75 to 0.75
- readout_bias: float32 [16, 4096], P('sess'), may hold values from -1 to 1
Outputs:
- loss: float32 [], replicated
- grad_conv_weight: float32 [64, 147], replicated
- grad_conv_bias: float32 [64], replicated
- grad_mix_weight: float32 [64, 64], replicated
- grad_mix_bias: float32 [64], replicated
- grad_masks: float32 [16, 4096, 576], P('sess', 'clip')
- grad_feat_w: float32 [16, 4096, 64], P('sess', 'clip')
- grad_readout_bias: float32 [16, 4096], P('sess', 'clip')
Inputs may be any that keep to these rules, and one draw needn't show every extreme that they name: `assignment`: in every aligned block of 16 clips, each of the 16 sessions is named by exactly one clip. `counts`: some session has exactly 4096 neurons.
All inputs are finite; a program needn't handle non-finite values.
Results may differ from a plain program's by a relative error of at most 0.0085.
Values may be sent and summed in bfloat16 or wider, within the bound.
A program may use at most 192 MiB of HBM per device.

v0:
```python
import functools

import jax
import jax.numpy as jnp
import numpy as np
from jax import lax
from jax.experimental import pallas as pl
from jax.experimental.pallas import tpu as pltpu
from jax.sharding import PartitionSpec as P

HH = 36
WW = 64
KS = 7
KT = 3
CH = 64
POOLED = 576
TAPS = 147
PLANES = 4
BASE_W = 768
ROWS = 16
NBLOCK = 512
GROWS = 648
F32 = jnp.float32
BF16 = jnp.bfloat16
VM = 56 * 2**20


def tap_tables():
    fold = np.zeros((4, 256, 256), np.float32)
    for a in range(2):
        for b in range(2):
            for dt in range(KT):
                for dy in range(KS):
                    for dx in range(KS):
                        u, v = dy + a, dx + b
                        depth = ((u // 2) * 4 + v // 2) * ROWS + dt * 4 + (u % 2) * 2 + v % 2
                        fold[a * 2 + b, depth, (dt * KS + dy) * KS + dx] = 1.0
            fold[a * 2 + b, 12, TAPS] = 1.0
    return fold


def split_table():
    table = np.zeros((512, 512), np.float32)
    for i in range(4):
        for ru in range(2):
            for x in range(WW):
                table[i * 128 + ru * 64 + x, (ru * 2 + x % 2) * 128 + i * 32 + x // 2] = 1.0
    return table


def dot(a, b, dims=((1,), (0,)), precision=None):
    return lax.dot_general(a, b, (dims, ((), ())), preferred_element_type=F32, precision=precision)


NT = ((1,), (1,))


def plane_offsets():
    return [66 - 32 * ru - rv for ru in (1, 0) for rv in (1, 0)]


def split_planes(video, table):
    blocks = [video[:, t * 512 : (t + 1) * 512] for t in range(4)]
    tail = jnp.concatenate([video[:, 2048:2304], jnp.zeros((16, 256), BF16)], axis=1)
    stacked = jnp.concatenate(blocks + [tail], axis=0)
    split = dot(stacked, table)
    out = []
    for plane, offset in enumerate(plane_offsets()):
        parts = [split[t * 16 : (t + 1) * 16, plane * 128 : (plane + 1) * 128] for t in range(5)]
        flat = jnp.concatenate(parts + [jnp.zeros((16, 128), F32)], axis=1)
        out.append(pltpu.roll(flat, offset, 1))
    return out[::-1]


def prep_kernel(video_ref, table_ref, planes_ref):
    planes = split_planes(video_ref[...], table_ref[...])
    planes_ref[...] = jnp.concatenate(planes, axis=0).astype(BF16)


def make_base(prev, own, after, tiled_assignment):
    stacked = jnp.concatenate([prev, own, after], axis=0)
    row = lax.broadcasted_iota(jnp.int32, (256, 192), 0)
    col = lax.broadcasted_iota(jnp.int32, (256, 192), 1)
    pick = (row % 16 == col // 16) & (tiled_assignment == row // 16)
    return dot(pick.astype(BF16), stacked)


def column_masks():
    row = lax.broadcasted_iota(jnp.int32, (ROWS, POOLED), 0)
    column = lax.broadcasted_iota(jnp.int32, (ROWS, POOLED), 1) % 32
    masks = []
    for shift in range(4):
        at = column + shift - 2 + row % 2
        masks.append((at >= 0) & (at < 32) & (row < 12))
    return masks


def fill_patches(base, patches_ref, masks):
    for qu in range(4):
        for qv in range(4):
            shift = qu * 32 + qv
            moved = base if shift == 0 else pltpu.roll(base, BASE_W - shift, 1)
            tile = jnp.where(masks[qv], moved[:, :POOLED], 0.0)
            if shift == 0:
                row = lax.broadcasted_iota(jnp.int32, (ROWS, POOLED), 0)
                tile = jnp.where(row == 12, 1.0, tile)
            at = (qu * 4 + qv) * ROWS
            patches_ref[at : at + ROWS, :] = tile.astype(BF16)


def conv_matrix(conv_weight, fold_ref, w2_ref):
    for ab in range(4):
        block = dot(conv_weight, fold_ref[ab].astype(BF16), NT)
        w2_ref[ab * CH : (ab + 1) * CH, :] = block.astype(BF16)


def activations(w2, patches, bias1, mix4, bias2):
    pre1 = dot(w2, patches) + bias1
    slope1 = jnp.exp(jnp.minimum(pre1, 0.0))
    act1 = jnp.where(pre1 > 0, pre1, slope1 - 1.0).astype(BF16)
    pre2 = dot(mix4, act1) + bias2
    slope2 = jnp.exp(jnp.minimum(pre2, 0.0))
    return slope1, act1, pre2, slope2


def forward_kernel(
    prev_ref, own_ref, after_ref, assign_ref, weight_ref, fold_ref, bias1_ref, mix_ref, bias2_ref,
    pooled_ref, base_ref, patches_ref, w2_ref,
):
    base_ref[...] = make_base(prev_ref[...], own_ref[...], after_ref[...], assign_ref[...])
    conv_matrix(weight_ref[...], fold_ref, w2_ref)
    masks = column_masks()

    def clip(k, carry):
        fill_patches(base_ref[pl.ds(pl.multiple_of(k * ROWS, ROWS), ROWS), :], patches_ref, masks)
        _, _, pre2, slope2 = activations(
            w2_ref[...], patches_ref[...], bias1_ref[...], mix_ref[...], bias2_ref[...]
        )
        feats = jnp.where(pre2 > 0, pre2, slope2 - 1.0).astype(BF16).astype(F32)
        total = feats[0:64] + feats[64:128] + feats[128:192] + feats[192:256]
        pooled_ref[k] = (total * 0.25).astype(BF16)
        return carry

    lax.fori_loop(0, 16, clip, 0)


def backward_kernel(
    prev_ref, own_ref, after_ref, assign_ref, weight_ref, fold_ref, bias1_ref, mix_ref, mix_t_ref, bias2_ref,
    grad_ref, loss_ref, small_ref, base_ref, patches_ref, w2_ref, gmix_ref, gconv_ref, gbias_ref,
):
    base_ref[...] = make_base(prev_ref[...], own_ref[...], after_ref[...], assign_ref[...])
    conv_matrix(weight_ref[...], fold_ref, w2_ref)
    masks = column_masks()
    gmix_ref[...] = jnp.zeros_like(gmix_ref)
    gconv_ref[...] = jnp.zeros_like(gconv_ref)
    gbias_ref[...] = jnp.zeros_like(gbias_ref)

    def clip(k, carry):
        fill_patches(base_ref[pl.ds(pl.multiple_of(k * ROWS, ROWS), ROWS), :], patches_ref, masks)
        patches = patches_ref[...]
        slope1, act1, _, slope2 = activations(
            w2_ref[...], patches, bias1_ref[...], mix_ref[...], bias2_ref[...]
        )
        grad = grad_ref[k].astype(F32) * 0.25
        grad4 = jnp.concatenate([grad] * 4, axis=0)
        pre2_grad = (grad4 * slope2).astype(BF16)
        gmix_ref[...] += dot(pre2_grad, act1, NT)
        gbias_ref[...] += jnp.sum(pre2_grad.astype(F32), axis=1, keepdims=True)
        pre1_grad = (dot(mix_t_ref[...], pre2_grad) * slope1).astype(BF16)
        gconv_ref[...] += dot(pre1_grad, patches, NT)
        return carry

    lax.fori_loop(0, 16, clip, 0)
    finish_small(gmix_ref, gconv_ref, gbias_ref, fold_ref, loss_ref[...], small_ref)


def finish_small(gmix_ref, gconv_ref, gbias_ref, fold_ref, loss, small_ref):
    row = lax.broadcasted_iota(jnp.int32, (256, 256), 0)
    col = lax.broadcasted_iota(jnp.int32, (256, 256), 1)
    total = jnp.zeros((CH, 256), F32)
    bias = jnp.zeros((CH, 1), F32)
    for ab in range(4):
        rows = slice(ab * CH, (ab + 1) * CH)
        place = ((row // CH == ab) & (col == row % CH + TAPS + 1)).astype(F32)
        total += dot(gconv_ref[rows, :], fold_ref[ab], precision=lax.Precision.HIGHEST)
        total += dot(gmix_ref[rows, :], place, precision=lax.Precision.HIGHEST)
        bias += gbias_ref[rows, :]
    lane = lax.broadcasted_iota(jnp.int32, (CH, 256), 1)
    line = lax.broadcasted_iota(jnp.int32, (CH, 256), 0)
    total = jnp.where(lane == TAPS + 1 + CH, bias, total)
    total = jnp.where((lane == TAPS + 2 + CH) & (line == 0), loss, total)
    small_ref[...] = total


def readout_kernel(
    loss_scale, count_ref, pooled_ref, mask_ref, weight_ref, rbias_ref, target_ref,
    grads_ref, back_ref, loss_ref, turned_ref, proj_ref, mixed_ref, total_ref,
):
    step = pl.program_id(0)

    @pl.when(step == 0)
    def _():
        turned_ref[...] = pooled_ref[...].T
        total_ref[...] = jnp.zeros_like(total_ref)
        loss_ref[...] = jnp.zeros_like(loss_ref)

    mask = mask_ref[...]
    weight = weight_ref[...].astype(F32).T
    proj_ref[...] = dot(pooled_ref[...], mask, NT)
    drives = []
    for f in range(16):
        drives.append(jnp.sum(proj_ref[f * CH : (f + 1) * CH, :] * weight, axis=0, keepdims=True))
    drive = jnp.concatenate(drives, axis=0) + rbias_ref[...]
    target = target_ref[...].astype(F32)
    small = jnp.exp(-jnp.abs(drive))
    rate = jnp.maximum(drive, 0.0) + jnp.log1p(small) + 0.1
    sigmoid = jnp.where(drive >= 0, 1.0, small) / (1.0 + small)
    slot = step * NBLOCK + lax.broadcasted_iota(jnp.int32, (16, NBLOCK), 1)
    alive = slot < count_ref[0]
    loss_ref[...] += jnp.sum(jnp.where(alive, rate - target * jnp.log(rate), 0.0), keepdims=True) * loss_scale
    grad_drive = jnp.where(alive, (1.0 - target / rate) * sigmoid, 0.0) * loss_scale
    feat = jnp.zeros((CH, NBLOCK), F32)
    for f in range(16):
        line = grad_drive[f : f + 1, :]
        feat += line * proj_ref[f * CH : (f + 1) * CH, :]
        mixed_ref[f * CH : (f + 1) * CH, :] = (line * weight).astype(BF16)
    grads_ref[0, POOLED : POOLED + CH, :] = feat
    bias_grad = jnp.sum(grad_drive, axis=0, keepdims=True)
    grads_ref[0, POOLED + CH : GROWS, :] = jnp.broadcast_to(bias_grad, (GROWS - POOLED - CH, NBLOCK))
    mixed = mixed_ref[...]
    grads_ref[0, 0:POOLED, :] = dot(turned_ref[...], mixed)
    total_ref[...] += dot(mixed, mask)

    @pl.when(step == pl.num_programs(0) - 1)
    def _():
        back_ref[...] = total_ref[...].astype(BF16)


def params():
    return pltpu.CompilerParams(vmem_limit_bytes=VM)


def run_prep(video, table):
    return pl.pallas_call(
        prep_kernel,
        out_shape=jax.ShapeDtypeStruct((64, BASE_W), BF16),
        compiler_params=params(),
        name="prep",
    )(video, table)


def run_forward(*args):
    return pl.pallas_call(
        forward_kernel,
        out_shape=jax.ShapeDtypeStruct((16, CH, POOLED), BF16),
        scratch_shapes=[
            pltpu.VMEM((256, BASE_W), F32),
            pltpu.VMEM((256, POOLED), BF16),
            pltpu.VMEM((256, 256), BF16),
        ],
        compiler_params=params(),
        name="core_forward",
    )(*args)


def run_backward(*args):
    return pl.pallas_call(
        backward_kernel,
        out_shape=jax.ShapeDtypeStruct((CH, 256), F32),
        scratch_shapes=[
            pltpu.VMEM((256, BASE_W), F32),
            pltpu.VMEM((256, POOLED), BF16),
            pltpu.VMEM((256, 256), BF16),
            pltpu.VMEM((256, 256), F32),
            pltpu.VMEM((256, 256), F32),
            pltpu.VMEM((256, 1), F32),
        ],
        compiler_params=params(),
        name="core_backward",
    )(*args)


def run_readout(loss_scale, count, pooled, masks, weight, rbias, target):
    neurons = masks.shape[0]
    steps = neurons // NBLOCK
    return pl.pallas_call(
        functools.partial(readout_kernel, loss_scale),
        grid=(steps,),
        in_specs=[
            pl.BlockSpec(memory_space=pltpu.SMEM),
            pl.BlockSpec((1024, POOLED), lambda i: (0, 0)),
            pl.BlockSpec((NBLOCK, POOLED), lambda i: (i, 0)),
            pl.BlockSpec((NBLOCK, CH), lambda i: (i, 0)),
            pl.BlockSpec((1, NBLOCK), lambda i: (0, i)),
            pl.BlockSpec((16, NBLOCK), lambda i: (0, i)),
        ],
        out_specs=[
            pl.BlockSpec((1, GROWS, NBLOCK), lambda i: (i, 0, 0)),
            pl.BlockSpec((1024, POOLED), lambda i: (0, 0)),
            pl.BlockSpec((1, 1), lambda i: (0, 0)),
        ],
        out_shape=[
            jax.ShapeDtypeStruct((steps, GROWS, NBLOCK), F32),
            jax.ShapeDtypeStruct((1024, POOLED), BF16),
            jax.ShapeDtypeStruct((1, 1), F32),
        ],
        scratch_shapes=[
            pltpu.VMEM((POOLED, 1024), BF16),
            pltpu.VMEM((1024, NBLOCK), F32),
            pltpu.VMEM((1024, NBLOCK), BF16),
            pltpu.VMEM((1024, POOLED), F32),
        ],
        compiler_params=params(),
        name="readout",
    )(count, pooled, masks, weight, rbias, target)


def per_device(
    video, responses, assignment, counts, conv_weight, conv_bias, mix_weight, mix_bias, masks, feat_w, readout_bias,
):
    sess_total = lax.axis_size("sess")
    clip_total = lax.axis_size("clip")
    loss_scale = 1.0 / (video.shape[0] * clip_total * sess_total)
    own = run_prep(video[:, 0, :], jnp.asarray(split_table(), BF16))
    up = [(i, i + 1) for i in range(sess_total - 1)]
    down = [(j, i) for i, j in up]
    prev = lax.ppermute(own, "sess", up)
    after = lax.ppermute(own, "sess", down)
    tiled_assignment = jnp.tile(assignment, 12)[None]
    pick = (assignment[None, :] == jnp.arange(16, dtype=jnp.int32)[:, None]).astype(BF16)
    target = jnp.dot(pick, responses[:, 0, :], preferred_element_type=F32).astype(BF16)
    target = lax.all_to_all(target, "sess", split_axis=0, concat_axis=0, tiled=True)
    weight = jnp.pad(conv_weight, ((0, 0), (0, 256 - TAPS)))
    fold = jnp.asarray(tap_tables())
    eye = jnp.eye(4, dtype=BF16)
    mix4 = jnp.kron(eye, mix_weight)
    mix4_t = jnp.kron(eye, mix_weight.T)
    bias1 = jnp.tile(conv_bias, 4)[:, None]
    bias2 = jnp.tile(mix_bias, 4)[:, None]
    core = (prev, own, after, tiled_assignment, weight, fold, bias1)
    pooled = run_forward(*core, mix4, bias2)
    received = lax.all_to_all(pooled, "sess", split_axis=0, concat_axis=0, tiled=True)
    grads, back, loss = run_readout(
        loss_scale, counts, received.reshape(1024, POOLED), masks[0], feat_w[0], readout_bias, target
    )
    summed = lax.psum_scatter(grads, "clip", scatter_dimension=0, tiled=True)
    returned = lax.all_to_all(back.reshape(16, CH, POOLED), "sess", split_axis=0, concat_axis=0, tiled=True)
    small = run_backward(*core, mix4, mix4_t, bias2, returned, loss)
    small = lax.psum(small, ("clip", "sess"))
    turned = summed[0].T
    return (
        small[0, TAPS + 2 + CH],
        small[:, :TAPS],
        small[:, TAPS],
        small[:, TAPS + 1 : TAPS + 1 + CH],
        small[:, TAPS + 1 + CH],
        turned[None, :, :POOLED],
        turned[None, :, POOLED : POOLED + CH],
        turned[None, :, POOLED + CH],
    )


def solution(mesh):
    return jax.shard_map(
        per_device,
        mesh=mesh,
        in_specs=(
            P("clip", "sess", None),
            P("clip", "sess", None),
            P("clip"),
            P("sess"),
            P(),
            P(),
            P(),
            P(),
            P("sess", None, None),
            P("sess", None, None),
            P("sess", None),
        ),
        out_specs=(
            P(),
            P(),
            P(),
            P(),
            P(),
            P("sess", "clip", None),
            P("sess", "clip", None),
            P("sess", "clip"),
        ),
        check_vma=False,
    )
```

profile of v0, /device:TPU:1, one launch (start us, length us, event | category | flops | bytes accessed | tf_op | source)
XLA Modules:
  0.0 326.0 jit_solution(17807591992977416657)
XLA Ops:
  8.1 2.0 prep.1.own_ref
  10.1 1.4 collective-permute-start.1
  11.5 4.6 %collective-permute-start = (bf16[64,768]{1,0:T(8,128)(2,1)}, bf16[64,768]{1,0:T(8,128)(2,1)S(1)}, u32[]{:S(2)}, u32[]{:S(2)}) collective-permute-start(bf16[64,768]{1,0:T(8,128)(2,1)} %prep.1.own_ref), channel_id=1, source_target_pairs={{0,1},{1,2},{2,3},{3,4},{4,5},{5,6},{6,7},{7,8},{8,9},{9,10},{10,1... | collective-permute-start | bytes 294920 | tf_op jit(solution)/shard_map/ppermute | solution.py:327
  18.9 9.5 %all-to-all-start.1 = ((bf16[16,2,2048]{2,1,0:T(2,128)(2,1)}), bf16[16,2,2048]{2,1,0:T(2,128)(2,1)S(1)}, u32[]{:S(2)}, u32[]{:S(2)}) async-start(bf16[16,2,2048]{2,1,0:T(2,128)(2,1)} %reshape.50), calls=%async_computation.1 | async-start | bytes 262144 | tf_op jit(solution)/shard_map/all_to_all | solution.py:332
  31.0 0.9 mul.44.mix_ref
  33.9 14.2 %core_forward.1 = bf16[16,64,576]{2,1,0:T(8,128)(2,1)} custom-call(bf16[64,768]{1,0:T(8,128)(2,1)} %copy-done.6, bf16[64,768]{1,0:T(8,128)(2,1)} %prep.1.own_ref, bf16[64,768]{1,0:T(8,128)(2,1)} %copy-done.5, s32[1,192]{1,0:T(1,128)} %broadcast_in_dim_tile.9.assign_ref, bf16[64,256]{1,0:T(8,128)(2,1)} %pad.4.weight_ref, ...), custom_call_target="tpu_custom_call" | custom-call | tf_op jit(solution)/shard_map/core_forward/pallas_call | solution.py:253
  48.1 6.8 %all-to-all-start = ((bf16[16,64,576]{2,1,0:T(8,128)(2,1)}), bf16[16,64,576]{2,1,0:T(8,128)(2,1)S(1)}, u32[]{:S(2)}, u32[]{:S(2)}) async-start(bf16[16,64,576]{2,1,0:T(8,128)(2,1)} %core_forward.1), calls=%async_computation | async-start | bytes 2621440 | tf_op jit(solution)/shard_map/all_to_all | solution.py:342
  55.5 1.3 copy.43
  56.8 7.6 %copy.42 = bf16[1,4096,576]{2,1,0:T(8,128)(2,1)} copy(bf16[1,4096,576]{1,2,0:T(8,128)(2,1)} %param.21) | data formatting | bytes 9437184 | tf_op args[8]
  65.4 7.1 %all-to-all-done = bf16[16,64,576]{2,1,0:T(8,128)(2,1)S(1)} async-done(((bf16[16,64,576]{2,1,0:T(8,128)(2,1)}), bf16[16,64,576]{2,1,0:T(8,128)(2,1)S(1)}, u32[]{:S(2)}, u32[]{:S(2)}) %all-to-all-start) | async-done | bytes 1179680 | tf_op jit(solution)/shard_map/all_to_all | solution.py:342
  72.5 1.0 copy-done.2
  73.6 26.6 %readout.1 = (f32[8,648,512]{2,1,0:T(8,128)}, bf16[1024,576]{1,0:T(8,128)(2,1)}, f32[1,1]{1,0:T(1,128)}) custom-call(s32[1]{0:T(128)S(6)} %copy.52.count_ref, bf16[1024,576]{1,0:T(8,128)(2,1)} %bitcast.26, bf16[4096,576]{1,0:T(8,128)(2,1)} %bitcast.25, bf16[4096,64]{1,0:T(8,128)(2,1)} %bitcast.27, f32[1,4096]{1,0:T(1,128)} %rbias_ref.1, ...), custom_call_target="tpu_custom_call" | custom-call | tf_op jit(solution)/shard_map/readout/pallas_call | solution.py:286
  100.2 5.2 %all-to-all-start.2 = ((bf16[16,64,576]{2,1,0:T(8,128)(2,1)}), bf16[16,64,576]{2,1,0:T(8,128)(2,1)S(1)}, u32[]{:S(2)}, u32[]{:S(2)}) async-start(bf16[16,64,576]{2,1,0:T(8,128)(2,1)} %bitcast.28), calls=%async_computation.2 | async-start | bytes 2621440 | tf_op jit(solution)/shard_map/all_to_all | solution.py:347
  105.5 0.9 mul.47.mix_t_ref
  106.4 16.6 %all-to-all-done.2.grad_ref = bf16[16,64,576]{2,1,0:T(8,128)(2,1)S(1)} async-done(((bf16[16,64,576]{2,1,0:T(8,128)(2,1)}), bf16[16,64,576]{2,1,0:T(8,128)(2,1)S(1)}, u32[]{:S(2)}, u32[]{:S(2)}) %all-to-all-start.2) | async-done | bytes 1179680 | tf_op jit(solution)/shard_map/all_to_all | solution.py:347
  123.0 1.1 copy-done.1
  124.0 21.4 %core_backward.1 = f32[64,256]{1,0:T(8,128)} custom-call(bf16[64,768]{1,0:T(8,128)(2,1)} %copy-done.6, bf16[64,768]{1,0:T(8,128)(2,1)} %prep.1.own_ref, bf16[64,768]{1,0:T(8,128)(2,1)} %copy-done.5, s32[1,192]{1,0:T(1,128)} %broadcast_in_dim_tile.9.assign_ref, bf16[64,256]{1,0:T(8,128)(2,1)} %pad.4.weight_ref, f32[4,256,256]{2,1,0:T(8,128)} %constant.8.clone.fold_ref, ...), custom_call_target="tpu_custom_call" | custom-call | tf_op jit(solution)/shard_map/core_backward/pallas_call | solution.py:267
  146.0 162.4 %all-reduce.3.cloned.1.call-done = f32[64,256]{1,0:T(8,128)} async-done(((f32[64,256]{1,0:T(8,128)}), f32[64,256]{1,0:T(8,128)}) %all-reduce.3.cloned.1.call-update) | async-done | bytes 65552 | tf_op jit(solution)/shard_map/psum | solution.py:349
  308.4 1.3 slice.32
  309.7 1.4 slice.35
  311.1 1.5 slice_reduce_fusion
  312.7 1.3 slice_bitcast_fusion.2
  314.0 1.6 slice_bitcast_fusion.1
  315.6 2.4 slice_bitcast_fusion
  (47 shorter events, 9.5 us)
Async XLA Ops:
  8.0 8.1 %copy-start = (bf16[16,1,4096]{2,0,1:T(8,128)(2,1)S(1)}, bf16[16,1,4096]{2,0,1:T(8,128)(2,1)}, u32[]{:S(2)}) copy-start(bf16[16,1,4096]{2,0,1:T(8,128)(2,1)} %param.14) | copy-start | bytes 393220
  8.0 20.8 %copy-start.9 = (s32[16]{0:T(128)S(1)}, s32[16]{0:T(128)}, u32[]{:S(2)}) copy-start(s32[16]{0:T(128)} %param.15) | copy-start | bytes 196
  8.0 20.4 %copy-start.7 = (bf16[64,64]{1,0:T(8,128)(2,1)S(1)}, bf16[64,64]{1,0:T(8,128)(2,1)}, u32[]{:S(2)}) copy-start(bf16[64,64]{1,0:T(8,128)(2,1)} %param.19) | copy-start | bytes 24580
  8.0 21.4 %copy-start.10 = (f32[64]{0:T(128)S(1)}, f32[64]{0:T(128)}, u32[]{:S(2)}) copy-start(f32[64]{0:T(128)} %param.20) | copy-start | bytes 772
  8.0 22.2 %copy-start.11 = (f32[64]{0:T(128)S(1)}, f32[64]{0:T(128)}, u32[]{:S(2)}) copy-start(f32[64]{0:T(128)} %param.18) | copy-start | bytes 772
  10.1 21.8 %copy-start.8 = (bf16[64,147]{1,0:T(8,128)(2,1)S(1)}, bf16[64,147]{1,0:T(8,128)(2,1)}, u32[]{:S(2)}) copy-start(bf16[64,147]{1,0:T(8,128)(2,1)} %param.17) | copy-start | bytes 56452
  10.1 22.5 %collective-permute-start.1 = (bf16[64,768]{1,0:T(8,128)(2,1)}, bf16[64,768]{1,0:T(8,128)(2,1)S(1)}, u32[]{:S(2)}, u32[]{:S(2)}) collective-permute-start(bf16[64,768]{1,0:T(8,128)(2,1)} %prep.1.own_ref), channel_id=1, source_target_pairs={{1,0},{2,1},{3,2},{4,3},{5,4},{6,5},{7,6},{8,7},{9,8},{10,9},{11,1... | collective-permute-start | bytes 294920 | tf_op jit(solution)/shard_map/ppermute | solution.py:328
  11.5 21.1 %collective-permute-start = (bf16[64,768]{1,0:T(8,128)(2,1)}, bf16[64,768]{1,0:T(8,128)(2,1)S(1)}, u32[]{:S(2)}, u32[]{:S(2)}) collective-permute-start(bf16[64,768]{1,0:T(8,128)(2,1)} %prep.1.own_ref), channel_id=1, source_target_pairs={{0,1},{1,2},{2,3},{3,4},{4,5},{5,6},{6,7},{7,8},{8,9},{9,10},{10,1... | collective-permute-start | bytes 294920 | tf_op jit(solution)/shard_map/ppermute | solution.py:327
  18.9 29.2 %all-to-all-start.1 = ((bf16[16,2,2048]{2,1,0:T(2,128)(2,1)}), bf16[16,2,2048]{2,1,0:T(2,128)(2,1)S(1)}, u32[]{:S(2)}, u32[]{:S(2)}) async-start(bf16[16,2,2048]{2,1,0:T(2,128)(2,1)} %reshape.50), calls=%async_computation.1 | async-start | bytes 262144 | tf_op jit(solution)/shard_map/all_to_all | solution.py:332
  32.6 0.7 copy-start.5
  33.2 0.6 copy-start.6
  48.0 7.5 %copy-start.3 = (bf16[1,4096,64]{1,2,0:T(8,128)(2,1)S(1)}, bf16[1,4096,64]{1,2,0:T(8,128)(2,1)}, u32[]{:S(2)}) copy-start(bf16[1,4096,64]{1,2,0:T(8,128)(2,1)} %param.22) | copy-start | bytes 1572868
  48.1 24.5 %all-to-all-start = ((bf16[16,64,576]{2,1,0:T(8,128)(2,1)}), bf16[16,64,576]{2,1,0:T(8,128)(2,1)S(1)}, u32[]{:S(2)}, u32[]{:S(2)}) async-start(bf16[16,64,576]{2,1,0:T(8,128)(2,1)} %core_forward.1), calls=%async_computation | async-start | bytes 2621440 | tf_op jit(solution)/shard_map/all_to_all | solution.py:342
  72.5 1.0 copy-start.2
  100.2 22.8 %all-to-all-start.2 = ((bf16[16,64,576]{2,1,0:T(8,128)(2,1)}), bf16[16,64,576]{2,1,0:T(8,128)(2,1)S(1)}, u32[]{:S(2)}, u32[]{:S(2)}) async-start(bf16[16,64,576]{2,1,0:T(8,128)(2,1)} %bitcast.28), calls=%async_computation.2 | async-start | bytes 2621440 | tf_op jit(solution)/shard_map/all_to_all | solution.py:347
  105.4 203.0 %all-reduce.3.cloned.1.call-start = ((), (), s32[]{:S(2)}) async-start(), calls=%async_computation.4 | async-start | bytes 131072 | tf_op jit(solution)/shard_map/psum | solution.py:349
  123.0 1.1 copy-start.1
  145.5 167.2 %reduce-scatter.2.cloned.1.call-start = ((), (), s32[]{:S(2)}) async-start(), calls=%async_computation.5 | async-start | bytes 11943936 | tf_op jit(solution)/shard_map/reduce_scatter | solution.py:346
  312.7 5.3 %copy-start.4 = (f32[64,256]{1,0:T(8,128)S(1)}, f32[64,256]{1,0:T(8,128)}, u32[]{:S(2)}) copy-start(f32[64,256]{1,0:T(8,128)} %all-reduce.3.cloned.1.call-done) | copy-start | bytes 196612
Sparse Core Ops, SparseCore 0:
  145.6 162.7 all-reduce.2
Sparse Core Ops, SparseCore 1:
  148.5 63.2 reduce-scatter.1
where the time goes:
time: 327 us; the launch traced here: 326 us
  waiting for transfers between devices  187 us (57%)
  Pallas kernels  64.2 us (20%)
  local copies, waits for them, and re-layouts  29.4 us (9%)
  starting transfers between devices  27.6 us (8%)
  between operations  16.3 us (5%)
    psum x1, waiting for transfers between devices, per_device(): small = lax.psum(small, ('clip', 'sess'))  162 us
    pallas_call x1, Pallas kernels, run_readout(): pl.pallas_call(functools.partial(readout_kernel, loss_scale), grid=(steps...  26.6 us
    pallas_call x1, Pallas kernels, run_backward(): pl.pallas_call(backward_kernel, out_shape=jax.ShapeDtypeStruct((CH, 256),...  21.4 us
    all_to_all x1, waiting for transfers between devices, per_device(): lax.all_to_all(back.reshape(16, CH, POOLED), 'sess', split_axis=0, concat...  16.6 us
    unnamed x30, local copies, waits for them, and re-layouts  14.7 us
    pallas_call x1, Pallas kernels, run_forward(): pl.pallas_call(forward_kernel, out_shape=jax.ShapeDtypeStruct((16, CH, PO...  14.2 us
    all_to_all x1, starting transfers between devices, per_device(): lax.all_to_all(target, 'sess', split_axis=0, concat_axis=0, tiled=True)  9.52 us
    all_to_all x1, waiting for transfers between devices, per_device(): lax.all_to_all(pooled, 'sess', split_axis=0, concat_axis=0, tiled=True)  7.11 us
  transfers between devices with their start and end apart: 7, of which 3 were waited for; matrix products, arithmetic and copies ran while one was open for 7% of the time, Pallas kernels for 4%

commit v1 on v0

v1 whole, which is shorter than its diff:
```python
import functools

import jax
import jax.numpy as jnp
import numpy as np
from jax import lax
from jax.experimental import pallas as pl
from jax.experimental.pallas import tpu as pltpu
from jax.sharding import PartitionSpec as P

HH = 36
WW = 64
KS = 7
KT = 3
CH = 64
POOLED = 576
TAPS = 147
BASE_W = 768
ROWS = 16
NBLOCK = 512
GROWS = 648
F32 = jnp.float32
BF16 = jnp.bfloat16
VM = 60 * 2**20
LOW = 328
MESH = pl.DeviceIdType.MESH


def tap_tables():
    fold = np.zeros((4, 256, 256), np.float32)
    for a in range(2):
        for b in range(2):
            for dt in range(KT):
                for dy in range(KS):
                    for dx in range(KS):
                        u, v = dy + a, dx + b
                        depth = ((u // 2) * 4 + v // 2) * ROWS + dt * 4 + (u % 2) * 2 + v % 2
                        fold[a * 2 + b, depth, (dt * KS + dy) * KS + dx] = 1.0
            fold[a * 2 + b, 12, TAPS] = 1.0
    return fold


def split_table():
    table = np.zeros((512, 512), np.float32)
    for i in range(4):
        for ru in range(2):
            for x in range(WW):
                table[i * 128 + ru * 64 + x, (ru * 2 + x % 2) * 128 + i * 32 + x // 2] = 1.0
    return table


def dot(a, b, dims=((1,), (0,)), precision=None):
    return lax.dot_general(a, b, (dims, ((), ())), preferred_element_type=F32, precision=precision)


NT = ((1,), (1,))


def plane_offsets():
    return [66 - 32 * ru - rv for ru in (1, 0) for rv in (1, 0)]


def split_planes(video, table):
    blocks = [video[:, t * 512 : (t + 1) * 512] for t in range(4)]
    tail = jnp.concatenate([video[:, 2048:2304], jnp.zeros((16, 256), BF16)], axis=1)
    stacked = jnp.concatenate(blocks + [tail], axis=0)
    split = dot(stacked, table)
    out = []
    for plane, offset in enumerate(plane_offsets()):
        parts = [split[t * 16 : (t + 1) * 16, plane * 128 : (plane + 1) * 128] for t in range(5)]
        flat = jnp.concatenate(parts + [jnp.zeros((16, 128), F32)], axis=1)
        out.append(pltpu.roll(flat, offset, 1))
    return out[::-1]


def column_masks():
    row = lax.broadcasted_iota(jnp.int32, (ROWS, POOLED), 0)
    column = lax.broadcasted_iota(jnp.int32, (ROWS, POOLED), 1) % 32
    masks = []
    for shift in range(4):
        at = column + shift - 2 + row % 2
        masks.append((at >= 0) & (at < 32) & (row < 12))
    return masks


def fill_patches(base, patches_ref, k, masks):
    for qu in range(4):
        for qv in range(4):
            shift = qu * 32 + qv
            moved = base if shift == 0 else pltpu.roll(base, BASE_W - shift, 1)
            tile = jnp.where(masks[qv], moved[:, :POOLED], 0.0)
            if shift == 0:
                row = lax.broadcasted_iota(jnp.int32, (ROWS, POOLED), 0)
                tile = jnp.where(row == 12, 1.0, tile)
            at = (qu * 4 + qv) * ROWS
            patches_ref[k, at : at + ROWS, :] = tile.astype(BF16)


def conv_matrix(conv_weight, fold_ref, w2_ref):
    for ab in range(4):
        block = dot(conv_weight, fold_ref[ab][:, :TAPS], NT)
        w2_ref[ab * CH : (ab + 1) * CH, :] = block.astype(BF16)


def remote(src, dst, sends, recvs, send_at, recv_at, peer):
    return pltpu.make_async_remote_copy(
        src_ref=src, dst_ref=dst, send_sem=sends.at[send_at], recv_sem=recvs.at[recv_at],
        device_id=peer, device_id_type=MESH,
    )


def iotas(shape):
    return lax.broadcasted_iota(jnp.int32, shape, 0), lax.broadcasted_iota(jnp.int32, shape, 1)


def one_hot(condition):
    return jnp.where(condition, 1.0, 0.0)


def sorting_matrix(assignment):
    row, _ = iotas((16, 16))
    pick = one_hot(assignment == row)
    row, col = iotas((16, 256))
    wide = dot(pick, one_hot(col % 16 == row))
    row, col = iotas((256, 16))
    tall = dot(one_hot(row // 16 == col), wide)
    row, col = iotas((256, 256))
    return jnp.where(row % 16 == col // 16, tall, 0.0).astype(BF16)


def column(line):
    row, col = iotas((CH, CH))
    one = jnp.sum(jnp.where(row == col, line, 0.0), axis=1, keepdims=True)
    return jnp.concatenate([one] * 4, axis=0)


def block_diagonal(matrix):
    row, col = iotas((CH, 256))
    wide = dot(matrix.astype(BF16), one_hot(col % CH == row).astype(BF16))
    row, col = iotas((256, 256))
    return jnp.where(row // CH == col // CH, jnp.concatenate([wide] * 4, axis=0), 0.0).astype(BF16)


def elu(values):
    return jnp.where(values > 0, values, jnp.exp(jnp.minimum(values, 0.0)) - 1.0)


def finish_small(gmix_ref, gconv_ref, gbias_ref, fold_ref, loss):
    row, col = iotas((256, 256))
    total = jnp.zeros((CH, 256), F32)
    bias = jnp.zeros((CH, 1), F32)
    for ab in range(4):
        rows = slice(ab * CH, (ab + 1) * CH)
        place = one_hot((row // CH == ab) & (col == row % CH + TAPS + 1))
        total += dot(gconv_ref[rows, :], fold_ref[ab].astype(F32), precision=lax.Precision.HIGHEST)
        total += dot(gmix_ref[rows, :], place, precision=lax.Precision.HIGHEST)
        bias += gbias_ref[rows, :]
    line, lane = iotas((CH, 256))
    total = jnp.where(lane == TAPS + 1 + CH, bias, total)
    return jnp.where((lane == TAPS + 2 + CH) & (line == 0), loss, total)


def step_kernel(
    loss_scale,
    count_ref, video_ref, responses_ref, assign_ref, weight_ref, bias1_ref, mix_ref, bias2_ref,
    masks_hbm, featw_hbm, rbias_ref, table_ref, fold_ref,
    loss_out, conv_out, convb_out, mix_out, mixb_out, gmask_out, gfeat_out, gbias_out,
    mask_ref, featw_ref, planes_ref, prev_ref, after_ref, base_ref, w2_ref, mix4_ref, mixt_ref,
    patches_ref, act_ref, feats_ref, psend_ref, precv_ref, tsend_ref, trecv_ref, target_ref,
    turned_ref, proj_ref, mixed_ref, total_ref, loss_ref,
    blocks_ref, got_ref, low_ref, up_ref, minus_ref, plus_ref, bsend_ref, brecv_ref,
    gmix_ref, gconv_ref, gmixb_ref, ar_ref, r1_ref, s2_ref, r2_ref, s3_ref, r3_ref,
    local_sem, halo_s, halo_r, pool_s, pool_r, targ_s, targ_r, pair_s, pair_r, ring_s, ring_r,
    back_s, back_r, a1_s, a1_r, a2_s, a2_r, a3_s, a3_r,
):
    sess = lax.axis_index("sess")
    clip = lax.axis_index("clip")
    row_y = clip // 2
    core = clip % 2

    mask_copy = pltpu.make_async_copy(masks_hbm.at[0], mask_ref, local_sem.at[0])
    featw_copy = pltpu.make_async_copy(featw_hbm.at[0], featw_ref, local_sem.at[1])
    mask_copy.start()
    featw_copy.start()

    barrier = pltpu.get_barrier_semaphore()

    def greet_sess(j, carry):
        pl.semaphore_signal(barrier, inc=1, device_id={"sess": (sess + j) % 16}, device_id_type=MESH)
        return carry

    def greet_clip(j, carry):
        pl.semaphore_signal(barrier, inc=1, device_id={"clip": (clip + j) % 8}, device_id_type=MESH)
        return carry

    lax.fori_loop(1, 16, greet_sess, 0)
    lax.fori_loop(1, 8, greet_clip, 0)

    planes = split_planes(video_ref[...], table_ref[...])
    planes_ref[...] = jnp.concatenate(planes, axis=0).astype(BF16)
    pl.semaphore_wait(barrier, 22)

    halo_up = remote(planes_ref, prev_ref, halo_s, halo_r, 0, 0, {"sess": (sess + 1) % 16})
    halo_down = remote(planes_ref, after_ref, halo_s, halo_r, 1, 1, {"sess": (sess + 15) % 16})
    halo_up.start()
    halo_down.start()

    sort = sorting_matrix(assign_ref[...])
    stacked = jnp.concatenate([responses_ref[:, q * 256 : (q + 1) * 256] for q in range(16)], axis=0)
    tsend_ref[...] = dot(sort, stacked).astype(BF16).reshape(16, 16, 256)

    def target_copy(j):
        peer = (sess + 1 + j) % 16
        return remote(tsend_ref.at[peer], trecv_ref.at[sess], targ_s, targ_r, peer, sess, {"sess": peer})

    def start_target(j, carry):
        target_copy(j).start()
        return carry

    lax.fori_loop(0, 15, start_target, 0)
    trecv_ref[sess] = tsend_ref[sess]

    conv_matrix(weight_ref[...], fold_ref, w2_ref)
    mix = mix_ref[...].astype(F32)
    mix4_ref[...] = block_diagonal(mix)
    mixt_ref[...] = block_diagonal(mix.T)
    bias1 = column(bias1_ref[...])
    bias2 = column(bias2_ref[...])
    masks = column_masks()

    halo_up.wait()
    halo_down.wait()
    none = jnp.zeros((64, BASE_W), BF16)
    prev = jnp.where(sess == 0, none, prev_ref[...])
    after = jnp.where(sess == 15, none, after_ref[...])
    window = jnp.concatenate([prev, planes_ref[...], after], axis=0)
    base_ref[...] = dot(sort[:, :192], window)

    def pooled_copy(j):
        peer = (sess + 1 + j) % 16
        return remote(psend_ref.at[peer], precv_ref.at[sess], pool_s, pool_r, peer, sess, {"sess": peer})

    def forward(j, carry):
        k = (sess + 1 + j) % 16
        fill_patches(base_ref[pl.ds(pl.multiple_of(k * ROWS, ROWS), ROWS), :], patches_ref, k, masks)
        act1 = elu(dot(w2_ref[...], patches_ref[k]) + bias1).astype(BF16)
        act_ref[k] = act1
        feats = elu(dot(mix4_ref[...], act1) + bias2).astype(BF16)
        feats_ref[k] = feats
        wide = feats.astype(F32)
        total = wide[0:64] + wide[64:128] + wide[128:192] + wide[192:256]
        psend_ref[k] = (total * 0.25).astype(BF16)

        @pl.when(j < 15)
        def _():
            pooled_copy(j).start()

        return carry

    lax.fori_loop(0, 16, forward, 0)
    precv_ref[sess] = psend_ref[sess]
    total_ref[...] = jnp.zeros_like(total_ref)
    loss_ref[...] = jnp.zeros_like(loss_ref)
    gmix_ref[...] = jnp.zeros_like(gmix_ref)
    gconv_ref[...] = jnp.zeros_like(gconv_ref)
    gmixb_ref[...] = jnp.zeros_like(gmixb_ref)
    mask_copy.wait()
    featw_copy.wait()

    def wait_forward(j, carry):
        peer = (sess + 15 - j) % 16
        there = (sess + 1 + j) % 16
        remote(psend_ref.at[there], precv_ref.at[peer], pool_s, pool_r, there, peer, {"sess": there}).wait()
        remote(tsend_ref.at[there], trecv_ref.at[peer], targ_s, targ_r, there, peer, {"sess": there}).wait()
        return carry

    lax.fori_loop(0, 15, wait_forward, 0)

    row, col = iotas((256, 256))
    swap = one_hot((row // 16 == col % 16) & (row % 16 == col // 16)).astype(BF16)
    target_ref[...] = dot(swap, trecv_ref[...].reshape(256, 256))
    turned_ref[...] = precv_ref[...].reshape(1024, POOLED).T

    partner = {"clip": row_y * 2 + 1 - core}
    right = {"clip": (row_y + 1) % 4 * 2 + core}
    left = {"clip": (row_y + 3) % 4 * 2 + core}
    high = GROWS - LOW

    def pair_copy(t):
        return remote(blocks_ref.at[t], got_ref.at[t], pair_s, pair_r, t, t, partner)

    def ring_copy(src, dst, at, peer):
        return remote(src, dst, ring_s, ring_r, at, at, peer)

    def lows(ref):
        return ref.at[pl.ds(0, LOW)]

    def highs(ref):
        return ref.at[pl.ds(LOW, high)]

    two = blocks_ref.at[4 + (row_y + 2) % 4]
    one = blocks_ref.at[4 + (row_y + 1) % 4]
    three = blocks_ref.at[4 + (row_y + 3) % 4]
    relay_low = ring_copy(lows(two), low_ref, 0, right)
    relay_high = ring_copy(highs(two), up_ref, 1, left)
    right_high = ring_copy(highs(one), highs(minus_ref), 2, right)
    left_low = ring_copy(lows(three), lows(plus_ref), 3, left)
    right_low = ring_copy(lows(one), lows(minus_ref), 4, right)
    left_high = ring_copy(highs(three), highs(plus_ref), 5, left)

    def readout(slot, n):
        mask = mask_ref[pl.ds(pl.multiple_of(n * NBLOCK, NBLOCK), NBLOCK), :]
        weight = featw_ref[pl.ds(pl.multiple_of(n * NBLOCK, NBLOCK), NBLOCK), :].astype(F32).T
        proj_ref[...] = dot(precv_ref[...].reshape(1024, POOLED), mask, NT)
        drives = []
        for f in range(16):
            drives.append(jnp.sum(proj_ref[f * CH : (f + 1) * CH, :] * weight, axis=0, keepdims=True))
        at = pl.ds(pl.multiple_of(n * NBLOCK, NBLOCK), NBLOCK)
        drive = jnp.concatenate(drives, axis=0) + rbias_ref[:, at]
        first = target_ref[pl.ds(pl.multiple_of(n * 32, 32), 16), :]
        second = target_ref[pl.ds(pl.multiple_of(n * 32 + 16, 16), 16), :]
        target = jnp.concatenate([first, second], axis=1)
        small = jnp.exp(-jnp.abs(drive))
        rate = jnp.maximum(drive, 0.0) + jnp.log1p(small) + 0.1
        sigmoid = jnp.where(drive >= 0, 1.0, small) / (1.0 + small)
        place = n * NBLOCK + lax.broadcasted_iota(jnp.int32, (16, NBLOCK), 1)
        alive = place < count_ref[0]
        terms = jnp.where(alive, rate - target * jnp.log(rate), 0.0)
        loss_ref[...] += jnp.sum(terms, keepdims=True) * loss_scale
        grad_drive = jnp.where(alive, (1.0 - target / rate) * sigmoid, 0.0) * loss_scale
        feat = jnp.zeros((CH, NBLOCK), F32)
        for f in range(16):
            line = grad_drive[f : f + 1, :]
            feat += line * proj_ref[f * CH : (f + 1) * CH, :]
            mixed_ref[f * CH : (f + 1) * CH, :] = (line * weight).astype(BF16)
        blocks_ref[slot, POOLED : POOLED + CH, :] = feat
        bias_grad = jnp.sum(grad_drive, axis=0, keepdims=True)
        blocks_ref[slot, POOLED + CH : GROWS, :] = jnp.broadcast_to(bias_grad, (GROWS - POOLED - CH, NBLOCK))
        mixed = mixed_ref[...]
        blocks_ref[slot, 0:POOLED, :] = dot(turned_ref[...], mixed)
        total_ref[...] += dot(mixed, mask)

    def phase(i, carry):
        t = (row_y + jnp.where(i == 0, 2, jnp.where(i == 1, 1, jnp.where(i == 2, 3, 0)))) % 4

        def half(h, inner):
            readout(h * 4 + t, t * 2 + jnp.where(h == 0, 1 - core, core))

            @pl.when(h == 0)
            def _():
                pair_copy(t).start()

            return inner

        lax.fori_loop(0, 2, half, 0)
        pair_copy(t).wait()
        blocks_ref[4 + t] += got_ref[t]

        @pl.when(i == 0)
        def _():
            relay_low.start()
            relay_high.start()

        @pl.when(i == 1)
        def _():
            right_high.start()

        @pl.when(i == 2)
        def _():
            left_low.start()

        return carry

    lax.fori_loop(0, 4, phase, 0)

    def back_copy(j):
        peer = (sess + 1 + j) % 16
        return remote(bsend_ref.at[peer], brecv_ref.at[sess], back_s, back_r, peer, sess, {"sess": peer})

    def send_back(j, carry):
        f = (sess + 1 + j) % 16
        bsend_ref[f] = total_ref[pl.ds(pl.multiple_of(f * CH, CH), CH), :].astype(BF16)

        @pl.when(j < 15)
        def _():
            back_copy(j).start()

        return carry

    lax.fori_loop(0, 16, send_back, 0)
    brecv_ref[sess] = bsend_ref[sess]

    relay_low.wait()
    blocks_ref[4 + (row_y + 1) % 4, 0:LOW, :] += low_ref[...]
    right_low.start()
    relay_high.wait()
    blocks_ref[4 + (row_y + 3) % 4, LOW:GROWS, :] += up_ref[...]
    left_high.start()

    def backward(j, carry):
        k = (sess + 15 - j) % 16
        there = (sess + 1 + j) % 16

        @pl.when(j < 15)
        def _():
            remote(bsend_ref.at[there], brecv_ref.at[k], back_s, back_r, there, k, {"sess": there}).wait()

        grad = brecv_ref[k].astype(F32) * 0.25
        slope2 = 1.0 + jnp.minimum(feats_ref[k].astype(F32), 0.0)
        pre2_grad = (jnp.concatenate([grad] * 4, axis=0) * slope2).astype(BF16)
        act1 = act_ref[k]
        gmix_ref[...] += dot(pre2_grad, act1, NT)
        gmixb_ref[...] += jnp.sum(pre2_grad.astype(F32), axis=1, keepdims=True)
        slope1 = 1.0 + jnp.minimum(act1.astype(F32), 0.0)
        pre1_grad = (dot(mixt_ref[...], pre2_grad) * slope1).astype(BF16)
        gconv_ref[...] += dot(pre1_grad, patches_ref[k], NT)
        return carry

    lax.fori_loop(0, 16, backward, 0)

    small = finish_small(gmix_ref, gconv_ref, gmixb_ref, fold_ref, loss_ref[...])
    for piece in range(16):
        top, lane = piece // 2 * 8, piece % 2 * 128
        ar_ref[piece] = small[top : top + 8, lane : lane + 128]

    def a1_copy(j, here):
        peer = (sess + 1 + j) % 16
        return remote(ar_ref.at[peer], r1_ref.at[here], a1_s, a1_r, peer, here, {"sess": peer})

    def a2_copy(j, here):
        peer = (clip + 1 + j) % 8
        return remote(s2_ref, r2_ref.at[here], a2_s, a2_r, peer, here, {"clip": peer})

    def a3_copy(j, here):
        peer = (sess + 1 + j) % 16
        return remote(s3_ref, r3_ref.at[here], a3_s, a3_r, peer, here, {"sess": peer})

    def exchange(copy, count, mine):
        def begin(j, carry):
            copy(j, mine).start()
            return carry

        def finish(j, carry):
            copy(j, (mine + count - j) % (count + 1)).wait()
            return carry

        lax.fori_loop(0, count, begin, 0)
        lax.fori_loop(0, count, finish, 0)

    r1_ref[sess] = ar_ref[sess]
    exchange(a1_copy, 15, sess)
    part = jnp.sum(r1_ref[...], axis=0)
    s2_ref[...] = part
    r2_ref[clip] = part
    exchange(a2_copy, 7, clip)
    part = jnp.sum(r2_ref[...], axis=0)
    s3_ref[...] = part
    r3_ref[sess] = part
    exchange(a3_copy, 15, sess)
    lines = [jnp.concatenate([r3_ref[2 * r], r3_ref[2 * r + 1]], axis=1) for r in range(8)]
    small = jnp.concatenate(lines, axis=0)
    conv_out[...] = small[:, :TAPS]
    row, col = iotas((CH, CH))
    convb_out[...] = jnp.sum(jnp.where(row == col, small[:, TAPS : TAPS + 1], 0.0), axis=0, keepdims=True)
    mix_out[...] = small[:, TAPS + 1 : TAPS + 1 + CH]
    mixb = small[:, TAPS + 1 + CH : TAPS + 2 + CH]
    mixb_out[...] = jnp.sum(jnp.where(row == col, mixb, 0.0), axis=0, keepdims=True)
    loss_out[...] = small[0:1, TAPS + 2 + CH : TAPS + 3 + CH]

    right_high.wait()
    left_low.wait()
    right_low.wait()
    left_high.wait()
    mine = blocks_ref[4 + row_y] + minus_ref[...] + plus_ref[...]
    gmask_out[...] = mine[0:POOLED].T
    gfeat_out[...] = mine[POOLED : POOLED + CH].T
    gbias_out[...] = mine[POOLED + CH : POOLED + CH + 1]


def run_step(loss_scale, *args):
    def vmem(shape, dtype):
        return pltpu.VMEM(shape, dtype)

    def dma(n):
        return pltpu.SemaphoreType.DMA((n,))

    whole = pl.BlockSpec(memory_space=pltpu.VMEM)
    anywhere = pl.BlockSpec(memory_space=pl.ANY)
    smem = pl.BlockSpec(memory_space=pltpu.SMEM)
    outs = [(1, 1), (CH, TAPS), (1, CH), (CH, CH), (1, CH), (NBLOCK, POOLED), (NBLOCK, CH), (1, NBLOCK)]
    neurons = args[8].shape[1]
    return pl.pallas_call(
        functools.partial(step_kernel, loss_scale),
        in_specs=[smem] + [whole] * 7 + [anywhere] * 2 + [whole] * 3,
        out_specs=[whole] * 8,
        out_shape=[jax.ShapeDtypeStruct(shape, F32) for shape in outs],
        scratch_shapes=[
            vmem((neurons, POOLED), BF16),
            vmem((neurons, CH), BF16),
            vmem((64, BASE_W), BF16),
            vmem((64, BASE_W), BF16),
            vmem((64, BASE_W), BF16),
            vmem((256, BASE_W), F32),
            vmem((256, 256), BF16),
            vmem((256, 256), BF16),
            vmem((256, 256), BF16),
            vmem((16, 256, POOLED), BF16),
            vmem((16, 256, POOLED), BF16),
            vmem((16, 256, POOLED), BF16),
            vmem((16, CH, POOLED), BF16),
            vmem((16, CH, POOLED), BF16),
            vmem((16, 16, 256), BF16),
            vmem((16, 16, 256), BF16),
            vmem((256, 256), F32),
            vmem((POOLED, 1024), BF16),
            vmem((1024, NBLOCK), F32),
            vmem((1024, NBLOCK), BF16),
            vmem((1024, POOLED), F32),
            vmem((1, 1), F32),
            vmem((8, GROWS, NBLOCK), F32),
            vmem((4, GROWS, NBLOCK), F32),
            vmem((LOW, NBLOCK), F32),
            vmem((GROWS - LOW, NBLOCK), F32),
            vmem((GROWS, NBLOCK), F32),
            vmem((GROWS, NBLOCK), F32),
            vmem((16, CH, POOLED), BF16),
            vmem((16, CH, POOLED), BF16),
            vmem((256, 256), F32),
            vmem((256, 256), F32),
            vmem((256, 1), F32),
            vmem((16, 8, 128), F32),
            vmem((16, 8, 128), F32),
            vmem((8, 128), F32),
            vmem((8, 8, 128), F32),
            vmem((8, 128), F32),
            vmem((16, 8, 128), F32),
        ]
        + [dma(n) for n in (2, 2, 2, 16, 16, 16, 16, 4, 4, 6, 6, 16, 16, 16, 16, 8, 8, 16, 16)],
        compiler_params=pltpu.CompilerParams(
            collective_id=0, has_side_effects=True, vmem_limit_bytes=VM
        ),
        name="train_step",
    )(*args)


def per_device(
    video, responses, assignment, counts, conv_weight, conv_bias, mix_weight, mix_bias, masks, feat_w, readout_bias,
):
    sess_total = lax.axis_size("sess")
    clip_total = lax.axis_size("clip")
    loss_scale = 1.0 / (video.shape[0] * clip_total * sess_total)
    loss, gconv, gconvb, gmix, gmixb, gmask, gfeat, gbias = run_step(
        loss_scale,
        counts,
        video.reshape(video.shape[0], -1),
        responses.reshape(responses.shape[0], -1),
        assignment[None],
        conv_weight,
        conv_bias[None],
        mix_weight,
        mix_bias[None],
        masks,
        feat_w,
        readout_bias,
        jnp.asarray(split_table(), BF16),
        jnp.asarray(tap_tables(), BF16),
    )
    return (
        loss[0, 0],
        gconv,
        gconvb[0],
        gmix,
        gmixb[0],
        gmask[None],
        gfeat[None],
        gbias,
    )


def solution(mesh):
    return jax.shard_map(
        per_device,
        mesh=mesh,
        in_specs=(
            P("clip", "sess", None),
            P("clip", "sess", None),
            P("clip"),
            P("sess"),
            P(),
            P(),
            P(),
            P(),
            P("sess", None, None),
            P("sess", None, None),
            P("sess", None),
        ),
        out_specs=(
            P(),
            P(),
            P(),
            P(),
            P(),
            P("sess", "clip", None),
            P("sess", "clip", None),
            P("sess", "clip"),
        ),
        check_vma=False,
    )
```

time: 327 us -> 128 us (0.39)
  waiting for transfers between devices: 187 us -> 0 us
  Pallas kernels: 64.2 us -> 103 us
  starting transfers between devices: 27.6 us -> 0 us
  between operations: 16.3 us -> 3.05 us
  local copies, waits for them, and re-layouts: 29.4 us -> 20.8 us
    psum x1 -> x0, waiting for transfers between devices: 162 us -> none  [per_device(): small = lax.psum(small, ('clip', 'sess'))]
    pallas_call x4 -> x1, Pallas kernels: 64.2 us -> 103 us  [run_step(): pl.pallas_call(functools.partial(step_kernel, loss_scale), in_specs=[smem...]
    all_to_all x3 -> x0, waiting for transfers between devices: 23.7 us -> none  [the longest x1 16.6 us: per_device(): lax.all_to_all(back.reshape(16, CH, POOLED), 'sess', split_axis=0, concat...]
    all_to_all x3 -> x0, starting transfers between devices: 21.6 us -> none  [the longest x1 9.52 us: per_device(): lax.all_to_all(target, 'sess', split_axis=0, concat_axis=0, tiled=True)]
    unnamed x30 -> x9, local copies, waits for them, and re-layouts: 14.7 us -> 20.8 us
    ppermute x2 -> x0, starting transfers between devices: 5.99 us -> none  [the longest x1 4.58 us: per_device(): prev = lax.ppermute(own, 'sess', up)]
    slice x3 -> x0, local copies, waits for them, and re-layouts: 4.25 us -> none  [the longest x1 1.54 us: per_device(): small[:, TAPS + 1 + CH]]
    broadcast_in_dim x2 -> x0, local copies, waits for them, and re-layouts: 3.93 us -> none  [the longest x1 2.36 us: per_device(): turned[None, :, :POOLED]]
  transfers between devices with their start and end apart: 7 -> 0, of which waited for: 3 -> 0; matrix products, arithmetic and copies ran while one was open for 7% -> 0% of each run, Pallas kernels for 4% -> 0%
where the time goes in v1:
time: 128 us; the launch traced here: 127 us
  Pallas kernels  103 us (80%)
  local copies, waits for them, and re-layouts  20.8 us (16%)
  between operations  3.05 us (2%)
    pallas_call x1, Pallas kernels, run_step(): pl.pallas_call(functools.partial(step_kernel, loss_scale), in_specs=[smem...  103 us
    unnamed x9, local copies, waits for them, and re-layouts  20.8 us

profile of v1, /device:TPU:1, one launch (start us, length us, event | category | flops | bytes accessed | tf_op | source)
XLA Modules:
  0.0 127.0 jit_solution(17611121296439972296)
XLA Ops:
  1.3 2.4 %copy.22.featw_hbm = bf16[1,4096,64]{2,1,0:T(8,128)(2,1)} copy(bf16[1,4096,64]{1,2,0:T(8,128)(2,1)} %param.22) | data formatting | bytes 1048576 | tf_op args[9]
  3.6 7.7 %copy.21.masks_hbm = bf16[1,4096,576]{2,1,0:T(8,128)(2,1)} copy(bf16[1,4096,576]{1,2,0:T(8,128)(2,1)} %param.21) | data formatting | bytes 9437184 | tf_op args[8]
  11.3 103.1 %train_step.1 = (f32[1,1]{1,0:T(1,128)}, f32[64,147]{1,0:T(8,128)}, f32[1,64]{1,0:T(1,128)}, f32[64,64]{1,0:T(8,128)}, f32[1,64]{1,0:T(1,128)}, /*index=5*/f32[5...) custom-call(s32[1]{0:T(128)S(6)} %copy.31.count_ref, bf16[16,2304]{1,0:T(8,128)(2,1)} %bitcast.13, ...), custom_call_target="tpu_custom_call" | custom-call | tf_op jit(solution)/shard_map/train_step/pallas_call | solution.py:492
  114.4 1.7 %copy.24 = f32[1,512,64]{1,2,0:T(8,128)} copy(f32[1,512,64]{2,1,0:T(8,128)} %bitcast.11) | data formatting | bytes 262144
  116.2 2.7 %copy.23 = f32[1,512,576]{1,2,0:T(8,128)} copy(f32[1,512,576]{2,1,0:T(8,128)} %bitcast.10) | data formatting | bytes 2359296
  119.5 1.5 %copy.33 = f32[64,147]{1,0:T(8,128)} copy(f32[64,147]{1,0:T(8,128)} %get-tuple-element.41) | data formatting | bytes 75264
  121.0 1.1 copy.34
  122.1 1.4 %copy.35 = f32[64,64]{1,0:T(8,128)} copy(f32[64,64]{1,0:T(8,128)} %get-tuple-element.43) | data formatting | bytes 32768
  123.5 1.1 copy.36
  124.6 1.2 copy.37

commit v2 on v1

--- a/solution.py
+++ b/solution.py
@@ -18,11 +18,12 @@
 BASE_W = 768
 ROWS = 16
 NBLOCK = 512
-GROWS = 648
+GROWS = 656
 F32 = jnp.float32
 BF16 = jnp.bfloat16
 VM = 60 * 2**20
-LOW = 328
+LOW = 336
+GROUP = 2
 MESH = pl.DeviceIdType.MESH
 
 
@@ -142,19 +143,18 @@
 
 
 def elu(values):
-    return jnp.where(values > 0, values, jnp.exp(jnp.minimum(values, 0.0)) - 1.0)
+    return jnp.maximum(values, jnp.exp(jnp.minimum(values, 0.0)) - 1.0)
 
 
 def finish_small(gmix_ref, gconv_ref, gbias_ref, fold_ref, loss):
     row, col = iotas((256, 256))
     total = jnp.zeros((CH, 256), F32)
-    bias = jnp.zeros((CH, 1), F32)
+    bias = jnp.sum(gbias_ref[...], axis=1, keepdims=True)
     for ab in range(4):
         rows = slice(ab * CH, (ab + 1) * CH)
         place = one_hot((row // CH == ab) & (col == row % CH + TAPS + 1))
         total += dot(gconv_ref[rows, :], fold_ref[ab].astype(F32), precision=lax.Precision.HIGHEST)
         total += dot(gmix_ref[rows, :], place, precision=lax.Precision.HIGHEST)
-        bias += gbias_ref[rows, :]
     line, lane = iotas((CH, 256))
     total = jnp.where(lane == TAPS + 1 + CH, bias, total)
     return jnp.where((lane == TAPS + 2 + CH) & (line == 0), loss, total)
@@ -164,11 +164,11 @@
     loss_scale,
     count_ref, video_ref, responses_ref, assign_ref, weight_ref, bias1_ref, mix_ref, bias2_ref,
     masks_hbm, featw_hbm, rbias_ref, table_ref, fold_ref,
-    loss_out, conv_out, convb_out, mix_out, mixb_out, gmask_out, gfeat_out, gbias_out,
+    small_out, grads_out,
     mask_ref, featw_ref, planes_ref, prev_ref, after_ref, base_ref, w2_ref, mix4_ref, mixt_ref,
     patches_ref, act_ref, feats_ref, psend_ref, precv_ref, tsend_ref, trecv_ref, target_ref,
     turned_ref, proj_ref, mixed_ref, total_ref, loss_ref,
-    blocks_ref, got_ref, low_ref, up_ref, minus_ref, plus_ref, bsend_ref, brecv_ref,
+    blocks_ref, got_ref, half_ref, low_ref, up_ref, minus_low_ref, minus_high_ref, plus_low_ref, plus_high_ref, bsend_ref, brecv_ref,
     gmix_ref, gconv_ref, gmixb_ref, ar_ref, r1_ref, s2_ref, r2_ref, s3_ref, r3_ref,
     local_sem, halo_s, halo_r, pool_s, pool_r, targ_s, targ_r, pair_s, pair_r, ring_s, ring_r,
     back_s, back_r, a1_s, a1_r, a2_s, a2_r, a3_s, a3_r,
@@ -240,24 +240,30 @@
         peer = (sess + 1 + j) % 16
         return remote(psend_ref.at[peer], precv_ref.at[sess], pool_s, pool_r, peer, sess, {"sess": peer})
 
-    def forward(j, carry):
-        k = (sess + 1 + j) % 16
-        fill_patches(base_ref[pl.ds(pl.multiple_of(k * ROWS, ROWS), ROWS), :], patches_ref, k, masks)
-        act1 = elu(dot(w2_ref[...], patches_ref[k]) + bias1).astype(BF16)
-        act_ref[k] = act1
-        feats = elu(dot(mix4_ref[...], act1) + bias2).astype(BF16)
-        feats_ref[k] = feats
-        wide = feats.astype(F32)
-        total = wide[0:64] + wide[64:128] + wide[128:192] + wide[192:256]
-        psend_ref[k] = (total * 0.25).astype(BF16)
-
-        @pl.when(j < 15)
-        def _():
-            pooled_copy(j).start()
-
-        return carry
-
-    lax.fori_loop(0, 16, forward, 0)
+    def forward(i, carry):
+        steps = [i * GROUP + g for g in range(GROUP)]
+        clips = [(sess + 1 + j) % 16 for j in steps]
+        for k in clips:
+            fill_patches(base_ref[pl.ds(pl.multiple_of(k * ROWS, ROWS), ROWS), :], patches_ref, k, masks)
+        pre1 = [dot(w2_ref[...], patches_ref[k]) for k in clips]
+        act1 = [elu(p + bias1).astype(BF16) for p in pre1]
+        pre2 = [dot(mix4_ref[...], a) for a in act1]
+        feats = [elu(p + bias2).astype(BF16) for p in pre2]
+        for k, a, f in zip(clips, act1, feats):
+            act_ref[k] = a
+            feats_ref[k] = f
+            wide = f.astype(F32)
+            total = (wide[0:64] + wide[64:128]) + (wide[128:192] + wide[192:256])
+            psend_ref[k] = (total * 0.25).astype(BF16)
+        for j in steps:
+
+            @pl.when(j < 15)
+            def _():
+                pooled_copy(j).start()
+
+        return carry
+
+    lax.fori_loop(0, 16 // GROUP, forward, 0)
     precv_ref[sess] = psend_ref[sess]
     total_ref[...] = jnp.zeros_like(total_ref)
     loss_ref[...] = jnp.zeros_like(loss_ref)
@@ -298,24 +304,24 @@
     def highs(ref):
         return ref.at[pl.ds(LOW, high)]
 
-    two = blocks_ref.at[4 + (row_y + 2) % 4]
-    one = blocks_ref.at[4 + (row_y + 1) % 4]
-    three = blocks_ref.at[4 + (row_y + 3) % 4]
-    relay_low = ring_copy(lows(two), low_ref, 0, right)
-    relay_high = ring_copy(highs(two), up_ref, 1, left)
-    right_high = ring_copy(highs(one), highs(minus_ref), 2, right)
-    left_low = ring_copy(lows(three), lows(plus_ref), 3, left)
-    right_low = ring_copy(lows(one), lows(minus_ref), 4, right)
-    left_high = ring_copy(highs(three), highs(plus_ref), 5, left)
+    at_two = 4 + (row_y + 2) % 4
+    at_one = 4 + (row_y + 1) % 4
+    at_three = 4 + (row_y + 3) % 4
+    relay_low = ring_copy(lows(half_ref.at[0]), low_ref, 0, right)
+    relay_high = ring_copy(highs(half_ref.at[0]), up_ref, 1, left)
+    right_high = ring_copy(highs(half_ref.at[1]), minus_high_ref, 2, right)
+    left_low = ring_copy(lows(half_ref.at[1]), plus_low_ref, 3, left)
+    right_low = ring_copy(lows(blocks_ref.at[at_one]), minus_low_ref, 4, right)
+    left_high = ring_copy(highs(blocks_ref.at[at_three]), plus_high_ref, 5, left)
 
     def readout(slot, n):
-        mask = mask_ref[pl.ds(pl.multiple_of(n * NBLOCK, NBLOCK), NBLOCK), :]
-        weight = featw_ref[pl.ds(pl.multiple_of(n * NBLOCK, NBLOCK), NBLOCK), :].astype(F32).T
-        proj_ref[...] = dot(precv_ref[...].reshape(1024, POOLED), mask, NT)
+        at = pl.ds(pl.multiple_of(n * NBLOCK, NBLOCK), NBLOCK)
+        mask = mask_ref[:, at]
+        weight = featw_ref[:, at].astype(F32)
+        proj_ref[...] = dot(precv_ref[...].reshape(1024, POOLED), mask)
         drives = []
         for f in range(16):
             drives.append(jnp.sum(proj_ref[f * CH : (f + 1) * CH, :] * weight, axis=0, keepdims=True))
-        at = pl.ds(pl.multiple_of(n * NBLOCK, NBLOCK), NBLOCK)
         drive = jnp.concatenate(drives, axis=0) + rbias_ref[:, at]
         first = target_ref[pl.ds(pl.multiple_of(n * 32, 32), 16), :]
         second = target_ref[pl.ds(pl.multiple_of(n * 32 + 16, 16), 16), :]
@@ -338,7 +344,7 @@
         blocks_ref[slot, POOLED + CH : GROWS, :] = jnp.broadcast_to(bias_grad, (GROWS - POOLED - CH, NBLOCK))
         mixed = mixed_ref[...]
         blocks_ref[slot, 0:POOLED, :] = dot(turned_ref[...], mixed)
-        total_ref[...] += dot(mixed, mask)
+        total_ref[...] += dot(mixed, mask, NT)
 
     def phase(i, carry):
         t = (row_y + jnp.where(i == 0, 2, jnp.where(i == 1, 1, jnp.where(i == 2, 3, 0)))) % 4
@@ -358,16 +364,25 @@
 
         @pl.when(i == 0)
         def _():
+            half_ref[0] = blocks_ref[at_two].astype(BF16)
             relay_low.start()
             relay_high.start()
 
         @pl.when(i == 1)
         def _():
+            half_ref[1, LOW:GROWS, :] = blocks_ref[at_one, LOW:GROWS, :].astype(BF16)
             right_high.start()
 
         @pl.when(i == 2)
         def _():
+            half_ref[1, 0:LOW, :] = blocks_ref[at_three, 0:LOW, :].astype(BF16)
             left_low.start()
+            relay_low.wait()
+            blocks_ref[at_one, 0:LOW, :] += low_ref[...].astype(F32)
+            right_low.start()
+            relay_high.wait()
+            blocks_ref[at_three, LOW:GROWS, :] += up_ref[...].astype(F32)
+            left_high.start()
 
         return carry
 
@@ -390,75 +405,92 @@
     lax.fori_loop(0, 16, send_back, 0)
     brecv_ref[sess] = bsend_ref[sess]
 
-    relay_low.wait()
-    blocks_ref[4 + (row_y + 1) % 4, 0:LOW, :] += low_ref[...]
-    right_low.start()
-    relay_high.wait()
-    blocks_ref[4 + (row_y + 3) % 4, LOW:GROWS, :] += up_ref[...]
-    left_high.start()
-
-    def backward(j, carry):
-        k = (sess + 15 - j) % 16
-        there = (sess + 1 + j) % 16
-
-        @pl.when(j < 15)
-        def _():
-            remote(bsend_ref.at[there], brecv_ref.at[k], back_s, back_r, there, k, {"sess": there}).wait()
-
-        grad = brecv_ref[k].astype(F32) * 0.25
-        slope2 = 1.0 + jnp.minimum(feats_ref[k].astype(F32), 0.0)
-        pre2_grad = (jnp.concatenate([grad] * 4, axis=0) * slope2).astype(BF16)
-        act1 = act_ref[k]
-        gmix_ref[...] += dot(pre2_grad, act1, NT)
-        gmixb_ref[...] += jnp.sum(pre2_grad.astype(F32), axis=1, keepdims=True)
-        slope1 = 1.0 + jnp.minimum(act1.astype(F32), 0.0)
-        pre1_grad = (dot(mixt_ref[...], pre2_grad) * slope1).astype(BF16)
-        gconv_ref[...] += dot(pre1_grad, patches_ref[k], NT)
-        return carry
-
-    lax.fori_loop(0, 16, backward, 0)
+    one_half = jnp.asarray(1.0, BF16)
+    zero_half = jnp.asarray(0.0, BF16)
+
+    def backward(i, carry):
+        steps = [i * GROUP + g for g in range(GROUP)]
+        clips = [(sess + 16 - m) % 16 for m in steps]
+        for m, k in zip(steps, clips):
+
+            @pl.when(m > 0)
+            def _():
+                there = (sess + m) % 16
+                remote(bsend_ref.at[there], brecv_ref.at[k], back_s, back_r, there, k, {"sess": there}).wait()
+
+        grads = [brecv_ref[k] * jnp.asarray(0.25, BF16) for k in clips]
+        slopes = [one_half + jnp.minimum(feats_ref[k], zero_half) for k in clips]
+        pre2_grad = [jnp.concatenate([g] * 4, axis=0) * s for g, s in zip(grads, slopes)]
+        act1 = [act_ref[k] for k in clips]
+        act1_grad = [dot(mixt_ref[...], p) for p in pre2_grad]
+        gmix_ref[...] += sum(dot(p, a, NT) for p, a in zip(pre2_grad, act1))
+        slopes = [(one_half + jnp.minimum(a, zero_half)).astype(F32) for a in act1]
+        pre1_grad = [(g * s).astype(BF16) for g, s in zip(act1_grad, slopes)]
+        wide = sum(p.astype(F32) for p in pre2_grad)
+        gmixb_ref[...] += (wide[0:64] + wide[64:128]) + (wide[128:192] + wide[192:256])
+        gconv_ref[...] += sum(dot(p, patches_ref[k], NT) for p, k in zip(pre1_grad, clips))
+        return carry
+
+    lax.fori_loop(0, 16 // GROUP, backward, 0)
 
     small = finish_small(gmix_ref, gconv_ref, gmixb_ref, fold_ref, loss_ref[...])
-    for piece in range(16):
-        top, lane = piece // 2 * 8, piece % 2 * 128
-        ar_ref[piece] = small[top : top + 8, lane : lane + 128]
+    for piece in range(8):
+        ar_ref[piece] = small[piece * 8 : piece * 8 + 8]
 
     def a1_copy(j, here):
+        peer = (clip + 1 + j) % 8
+        return remote(ar_ref.at[peer], r1_ref.at[here], a1_s, a1_r, peer, here, {"clip": peer})
+
+    def a2_copy(j, here):
         peer = (sess + 1 + j) % 16
-        return remote(ar_ref.at[peer], r1_ref.at[here], a1_s, a1_r, peer, here, {"sess": peer})
-
-    def a2_copy(j, here):
+        return remote(s2_ref, r2_ref.at[here], a2_s, a2_r, peer, here, {"sess": peer})
+
+    def a3_copy(j, here):
         peer = (clip + 1 + j) % 8
-        return remote(s2_ref, r2_ref.at[here], a2_s, a2_r, peer, here, {"clip": peer})
-
-    def a3_copy(j, here):
-        peer = (sess + 1 + j) % 16
-        return remote(s3_ref, r3_ref.at[here], a3_s, a3_r, peer, here, {"sess": peer})
-
-    def exchange(copy, count, mine):
+        return remote(s3_ref, r3_ref.at[here], a3_s, a3_r, peer, here, {"clip": peer})
+
+    def begin_all(copy, count, mine):
         def begin(j, carry):
             copy(j, mine).start()
             return carry
 
+        lax.fori_loop(0, count, begin, 0)
+
+    def finish_all(copy, count, mine):
         def finish(j, carry):
             copy(j, (mine + count - j) % (count + 1)).wait()
             return carry
 
-        lax.fori_loop(0, count, begin, 0)
         lax.fori_loop(0, count, finish, 0)
 
-    r1_ref[sess] = ar_ref[sess]
-    exchange(a1_copy, 15, sess)
+    begin_all(a1_copy, 7, clip)
+    r1_ref[clip] = ar_ref[clip]
+    finish_all(a1_copy, 7, clip)
     part = jnp.sum(r1_ref[...], axis=0)
     s2_ref[...] = part
-    r2_ref[clip] = part
-    exchange(a2_copy, 7, clip)
+    begin_all(a2_copy, 15, sess)
+    r2_ref[sess] = part
+    finish_all(a2_copy, 15, sess)
     part = jnp.sum(r2_ref[...], axis=0)
     s3_ref[...] = part
-    r3_ref[sess] = part
-    exchange(a3_copy, 15, sess)
-    lines = [jnp.concatenate([r3_ref[2 * r], r3_ref[2 * r + 1]], axis=1) for r in range(8)]
-    small = jnp.concatenate(lines, axis=0)
+    begin_all(a3_copy, 7, clip)
+    r3_ref[clip] = part
+    right_high.wait()
+    left_low.wait()
+    right_low.wait()
+    left_high.wait()
+    low = blocks_ref[4 + row_y, 0:LOW, :] + minus_low_ref[...]
+    grads_out[0:LOW, :] = low + plus_low_ref[...].astype(F32)
+    top = blocks_ref[4 + row_y, LOW:GROWS, :] + plus_high_ref[...]
+    grads_out[LOW:GROWS, :] = top + minus_high_ref[...].astype(F32)
+    finish_all(a3_copy, 7, clip)
+    small_out[...] = r3_ref[...].reshape(CH, 256)
+
+
+def split_kernel(
+    small_ref, grads_ref, loss_out, conv_out, convb_out, mix_out, mixb_out, gmask_out, gfeat_out, gbias_out
+):
+    small = small_ref[...]
     conv_out[...] = small[:, :TAPS]
     row, col = iotas((CH, CH))
     convb_out[...] = jnp.sum(jnp.where(row == col, small[:, TAPS : TAPS + 1], 0.0), axis=0, keepdims=True)
@@ -466,15 +498,18 @@
     mixb = small[:, TAPS + 1 + CH : TAPS + 2 + CH]
     mixb_out[...] = jnp.sum(jnp.where(row == col, mixb, 0.0), axis=0, keepdims=True)
     loss_out[...] = small[0:1, TAPS + 2 + CH : TAPS + 3 + CH]
-
-    right_high.wait()
-    left_low.wait()
-    right_low.wait()
-    left_high.wait()
-    mine = blocks_ref[4 + row_y] + minus_ref[...] + plus_ref[...]
-    gmask_out[...] = mine[0:POOLED].T
-    gfeat_out[...] = mine[POOLED : POOLED + CH].T
-    gbias_out[...] = mine[POOLED + CH : POOLED + CH + 1]
+    gmask_out[...] = grads_ref[0:POOLED]
+    gfeat_out[...] = grads_ref[POOLED : POOLED + CH]
+    gbias_out[...] = grads_ref[POOLED + CH : POOLED + CH + 1]
+
+
+def run_split(small, grads):
+    outs = [(1, 1), (CH, TAPS), (1, CH), (CH, CH), (1, CH), (POOLED, NBLOCK), (CH, NBLOCK), (1, NBLOCK)]
+    return pl.pallas_call(
+        split_kernel,
+        out_shape=[jax.ShapeDtypeStruct(shape, F32) for shape in outs],
+        name="split_results",
+    )(small, grads)
 
 
 def run_step(loss_scale, *args):
@@ -487,16 +522,16 @@
     whole = pl.BlockSpec(memory_space=pltpu.VMEM)
     anywhere = pl.BlockSpec(memory_space=pl.ANY)
     smem = pl.BlockSpec(memory_space=pltpu.SMEM)
-    outs = [(1, 1), (CH, TAPS), (1, CH), (CH, CH), (1, CH), (NBLOCK, POOLED), (NBLOCK, CH), (1, NBLOCK)]
-    neurons = args[8].shape[1]
+    outs = [(CH, 256), (GROWS, NBLOCK)]
+    neurons = args[8].shape[2]
     return pl.pallas_call(
         functools.partial(step_kernel, loss_scale),
         in_specs=[smem] + [whole] * 7 + [anywhere] * 2 + [whole] * 3,
-        out_specs=[whole] * 8,
+        out_specs=[whole] * 2,
         out_shape=[jax.ShapeDtypeStruct(shape, F32) for shape in outs],
         scratch_shapes=[
-            vmem((neurons, POOLED), BF16),
-            vmem((neurons, CH), BF16),
+            vmem((POOLED, neurons), BF16),
+            vmem((CH, neurons), BF16),
             vmem((64, BASE_W), BF16),
             vmem((64, BASE_W), BF16),
             vmem((64, BASE_W), BF16),
@@ -519,23 +554,26 @@
             vmem((1, 1), F32),
             vmem((8, GROWS, NBLOCK), F32),
             vmem((4, GROWS, NBLOCK), F32),
+            vmem((2, GROWS, NBLOCK), BF16),
+            vmem((LOW, NBLOCK), BF16),
+            vmem((GROWS - LOW, NBLOCK), BF16),
             vmem((LOW, NBLOCK), F32),
+            vmem((GROWS - LOW, NBLOCK), BF16),
+            vmem((LOW, NBLOCK), BF16),
             vmem((GROWS - LOW, NBLOCK), F32),
-            vmem((GROWS, NBLOCK), F32),
-            vmem((GROWS, NBLOCK), F32),
             vmem((16, CH, POOLED), BF16),
             vmem((16, CH, POOLED), BF16),
             vmem((256, 256), F32),
             vmem((256, 256), F32),
-            vmem((256, 1), F32),
-            vmem((16, 8, 128), F32),
-            vmem((16, 8, 128), F32),
-            vmem((8, 128), F32),
-            vmem((8, 8, 128), F32),
-            vmem((8, 128), F32),
-            vmem((16, 8, 128), F32),
+            vmem((CH, POOLED), F32),
+            vmem((8, 8, 256), F32),
+            vmem((8, 8, 256), F32),
+            vmem((8, 256), F32),
+            vmem((16, 8, 256), F32),
+            vmem((8, 256), F32),
+            vmem((8, 8, 256), F32),
         ]
-        + [dma(n) for n in (2, 2, 2, 16, 16, 16, 16, 4, 4, 6, 6, 16, 16, 16, 16, 8, 8, 16, 16)],
+        + [dma(n) for n in (2, 2, 2, 16, 16, 16, 16, 4, 4, 6, 6, 16, 16, 8, 8, 16, 16, 8, 8)],
         compiler_params=pltpu.CompilerParams(
             collective_id=0, has_side_effects=True, vmem_limit_bytes=VM
         ),
@@ -549,7 +587,7 @@
     sess_total = lax.axis_size("sess")
     clip_total = lax.axis_size("clip")
     loss_scale = 1.0 / (video.shape[0] * clip_total * sess_total)
-    loss, gconv, gconvb, gmix, gmixb, gmask, gfeat, gbias = run_step(
+    small, grads = run_step(
         loss_scale,
         counts,
         video.reshape(video.shape[0], -1),
@@ -559,20 +597,21 @@
         conv_bias[None],
         mix_weight,
         mix_bias[None],
-        masks,
-        feat_w,
+        jnp.swapaxes(masks, 1, 2),
+        jnp.swapaxes(feat_w, 1, 2),
         readout_bias,
         jnp.asarray(split_table(), BF16),
         jnp.asarray(tap_tables(), BF16),
     )
+    loss, gconv, gconvb, gmix, gmixb, gmask, gfeat, gbias = run_split(small, grads)
     return (
         loss[0, 0],
         gconv,
         gconvb[0],
         gmix,
         gmixb[0],
-        gmask[None],
-        gfeat[None],
+        gmask.T[None],
+        gfeat.T[None],
         gbias,
     )
 

time: 128 us -> 101 us (0.79)
  local copies, waits for them, and re-layouts: 20.8 us -> 0 us
  Pallas kernels: 103 us -> 99.9 us
  between operations: 3.05 us -> 1.29 us
    unnamed x9 -> x0, local copies, waits for them, and re-layouts: 20.8 us -> none
    pallas_call x1, Pallas kernels: 103 us -> 97.4 us  [run_step(): pl.pallas_call(functools.partial(step_kernel, loss_scale), in_specs=[smem...]
    pallas_call x0 -> x1, Pallas kernels: none -> 2.51 us  [run_split(): pl.pallas_call(split_kernel, out_shape=[jax.ShapeDtypeStruct(shape, F32)...]
where the time goes in v2:
time: 101 us
  Pallas kernels  99.9 us (99%)
  between operations  1.29 us (1%)
    pallas_call x1, Pallas kernels, run_step(): pl.pallas_call(functools.partial(step_kernel, loss_scale), in_specs=[smem...  97.4 us
    pallas_call x1, Pallas kernels, run_split(): pl.pallas_call(split_kernel, out_shape=[jax.ShapeDtypeStruct(shape, F32)...  2.51 us

profile of v2, /device:TPU:1, one launch (start us, length us, event | category | flops | bytes accessed | tf_op | source)
XLA Modules:
  0.0 101.2 jit_solution(9818341771921819396)
XLA Ops:
  1.3 97.4 %train_step.1 = (f32[64,256]{1,0:T(8,128)}, f32[656,512]{1,0:T(8,128)}) custom-call(s32[1]{0:T(128)S(6)} %copy.21.count_ref, bf16[16,2304]{1,0:T(8,128)(2,1)} %bitcast.19, bf16[16,4096]{1,0:T(8,128)(2,1)} %bitcast.18, s32[1,16]{1,0:T(1,128)} %bitcast.20, bf16[64,147]{1,0:T(8,128)(2,1)} %weight_ref.1, f32[1,64]{1,0:T(1,128)} %bitcast.21, ...), custom_call_target="tpu_custom_call" | custom-call | tf_op jit(solution)/shard_map/train_step/pallas_call | solution.py:527
  98.7 2.5 %split_results.1 = (f32[1,1]{1,0:T(1,128)}, f32[64,147]{1,0:T(8,128)}, f32[1,64]{1,0:T(1,128)}, f32[64,64]{1,0:T(8,128)}, f32[1,64]{1,0:T(1,128)}, /*index=5*/f3...) custom-call(f32[64,256]{1,0:T(8,128)} %get-tuple-element.18.small_ref, f32[656,512]{1,0:T(8,128)} %get-tuple-element.19.grads_ref), custom_call_target="tpu_custom_call" | custom-call | tf_op jit(solution)/shard_map/split_results/pallas_call | solution.py:508

commit v3 on v2

--- a/solution.py
+++ b/solution.py
@@ -24,6 +24,8 @@
 VM = 60 * 2**20
 LOW = 336
 GROUP = 2
+HALF = 8
+RELAY_AT = 2
 MESH = pl.DeviceIdType.MESH
 
 
@@ -183,6 +185,18 @@
     mask_copy.start()
     featw_copy.start()
 
+    def shift(m):
+        dz = m % 8 // 2
+        return dz, m % 2 * 2 + (dz + m // 8) % 2
+
+    def target_of(m):
+        dz, dx = shift(m)
+        return (sess // 4 + dz) % 4 * 4 + (sess + dx) % 4
+
+    def source_of(m):
+        dz, dx = shift(m)
+        return (sess // 4 + 4 - dz) % 4 * 4 + (sess + 4 - dx) % 4
+
     barrier = pltpu.get_barrier_semaphore()
 
     def greet_sess(j, carry):
@@ -209,16 +223,16 @@
     stacked = jnp.concatenate([responses_ref[:, q * 256 : (q + 1) * 256] for q in range(16)], axis=0)
     tsend_ref[...] = dot(sort, stacked).astype(BF16).reshape(16, 16, 256)
 
-    def target_copy(j):
-        peer = (sess + 1 + j) % 16
-        return remote(tsend_ref.at[peer], trecv_ref.at[sess], targ_s, targ_r, peer, sess, {"sess": peer})
-
-    def start_target(j, carry):
-        target_copy(j).start()
-        return carry
-
-    lax.fori_loop(0, 15, start_target, 0)
-    trecv_ref[sess] = tsend_ref[sess]
+    def target_copy(m):
+        peer = target_of(m)
+        return remote(tsend_ref.at[peer], trecv_ref.at[m], targ_s, targ_r, m, m, {"sess": peer})
+
+    def start_target(m, carry):
+        target_copy(m).start()
+        return carry
+
+    lax.fori_loop(1, 16, start_target, 0)
+    trecv_ref[0] = tsend_ref[sess]
 
     conv_matrix(weight_ref[...], fold_ref, w2_ref)
     mix = mix_ref[...].astype(F32)
@@ -236,13 +250,13 @@
     window = jnp.concatenate([prev, planes_ref[...], after], axis=0)
     base_ref[...] = dot(sort[:, :192], window)
 
-    def pooled_copy(j):
-        peer = (sess + 1 + j) % 16
-        return remote(psend_ref.at[peer], precv_ref.at[sess], pool_s, pool_r, peer, sess, {"sess": peer})
+    def pooled_copy(m):
+        peer = target_of(m)
+        return remote(psend_ref.at[peer], precv_ref.at[m], pool_s, pool_r, m, m, {"sess": peer})
 
     def forward(i, carry):
         steps = [i * GROUP + g for g in range(GROUP)]
-        clips = [(sess + 1 + j) % 16 for j in steps]
+        clips = [target_of((j + 1) % 16) for j in steps]
         for k in clips:
             fill_patches(base_ref[pl.ds(pl.multiple_of(k * ROWS, ROWS), ROWS), :], patches_ref, k, masks)
         pre1 = [dot(w2_ref[...], patches_ref[k]) for k in clips]
@@ -259,12 +273,12 @@
 
             @pl.when(j < 15)
             def _():
-                pooled_copy(j).start()
+                pooled_copy(j + 1).start()
 
         return carry
 
     lax.fori_loop(0, 16 // GROUP, forward, 0)
-    precv_ref[sess] = psend_ref[sess]
+    precv_ref[0] = psend_ref[sess]
     total_ref[...] = jnp.zeros_like(total_ref)
     loss_ref[...] = jnp.zeros_like(loss_ref)
     gmix_ref[...] = jnp.zeros_like(gmix_ref)
@@ -273,19 +287,18 @@
     mask_copy.wait()
     featw_copy.wait()
 
-    def wait_forward(j, carry):
-        peer = (sess + 15 - j) % 16
-        there = (sess + 1 + j) % 16
-        remote(psend_ref.at[there], precv_ref.at[peer], pool_s, pool_r, there, peer, {"sess": there}).wait()
-        remote(tsend_ref.at[there], trecv_ref.at[peer], targ_s, targ_r, there, peer, {"sess": there}).wait()
-        return carry
-
-    lax.fori_loop(0, 15, wait_forward, 0)
-
+    def wait_pooled(m, carry):
+        pooled_copy(m).wait()
+        return carry
+
+    def wait_target(m, carry):
+        target_copy(m).wait()
+        return carry
+
+    lax.fori_loop(1, 16, wait_target, 0)
     row, col = iotas((256, 256))
     swap = one_hot((row // 16 == col % 16) & (row % 16 == col // 16)).astype(BF16)
     target_ref[...] = dot(swap, trecv_ref[...].reshape(256, 256))
-    turned_ref[...] = precv_ref[...].reshape(1024, POOLED).T
 
     partner = {"clip": row_y * 2 + 1 - core}
     right = {"clip": (row_y + 1) % 4 * 2 + core}
@@ -314,43 +327,85 @@
     right_low = ring_copy(lows(blocks_ref.at[at_one]), minus_low_ref, 4, right)
     left_high = ring_copy(highs(blocks_ref.at[at_three]), plus_high_ref, 5, left)
 
-    def readout(slot, n):
+    def readout(slot, n, half):
         at = pl.ds(pl.multiple_of(n * NBLOCK, NBLOCK), NBLOCK)
+        frames = slice(half * HALF, (half + 1) * HALF)
+        rows = slice(half * HALF * CH, (half + 1) * HALF * CH)
         mask = mask_ref[:, at]
         weight = featw_ref[:, at].astype(F32)
-        proj_ref[...] = dot(precv_ref[...].reshape(1024, POOLED), mask)
+        proj_ref[...] = dot(precv_ref[frames].reshape(HALF * CH, POOLED), mask)
         drives = []
-        for f in range(16):
+        for f in range(HALF):
             drives.append(jnp.sum(proj_ref[f * CH : (f + 1) * CH, :] * weight, axis=0, keepdims=True))
         drive = jnp.concatenate(drives, axis=0) + rbias_ref[:, at]
-        first = target_ref[pl.ds(pl.multiple_of(n * 32, 32), 16), :]
-        second = target_ref[pl.ds(pl.multiple_of(n * 32 + 16, 16), 16), :]
+        first = target_ref[pl.ds(pl.multiple_of(n * 32 + half * HALF, HALF), HALF), :]
+        second = target_ref[pl.ds(pl.multiple_of(n * 32 + 16 + half * HALF, HALF), HALF), :]
         target = jnp.concatenate([first, second], axis=1)
         small = jnp.exp(-jnp.abs(drive))
         rate = jnp.maximum(drive, 0.0) + jnp.log1p(small) + 0.1
         sigmoid = jnp.where(drive >= 0, 1.0, small) / (1.0 + small)
-        place = n * NBLOCK + lax.broadcasted_iota(jnp.int32, (16, NBLOCK), 1)
+        place = n * NBLOCK + lax.broadcasted_iota(jnp.int32, (HALF, NBLOCK), 1)
         alive = place < count_ref[0]
         terms = jnp.where(alive, rate - target * jnp.log(rate), 0.0)
         loss_ref[...] += jnp.sum(terms, keepdims=True) * loss_scale
         grad_drive = jnp.where(alive, (1.0 - target / rate) * sigmoid, 0.0) * loss_scale
         feat = jnp.zeros((CH, NBLOCK), F32)
-        for f in range(16):
+        for f in range(HALF):
             line = grad_drive[f : f + 1, :]
             feat += line * proj_ref[f * CH : (f + 1) * CH, :]
             mixed_ref[f * CH : (f + 1) * CH, :] = (line * weight).astype(BF16)
-        blocks_ref[slot, POOLED : POOLED + CH, :] = feat
         bias_grad = jnp.sum(grad_drive, axis=0, keepdims=True)
-        blocks_ref[slot, POOLED + CH : GROWS, :] = jnp.broadcast_to(bias_grad, (GROWS - POOLED - CH, NBLOCK))
+        bias_grad = jnp.broadcast_to(bias_grad, (GROWS - POOLED - CH, NBLOCK))
         mixed = mixed_ref[...]
-        blocks_ref[slot, 0:POOLED, :] = dot(turned_ref[...], mixed)
-        total_ref[...] += dot(mixed, mask, NT)
+        mask_grad = dot(turned_ref[...], mixed)
+        if half == 0:
+            blocks_ref[slot, 0:POOLED, :] = mask_grad
+            blocks_ref[slot, POOLED : POOLED + CH, :] = feat
+            blocks_ref[slot, POOLED + CH : GROWS, :] = bias_grad
+        else:
+            blocks_ref[slot, 0:POOLED, :] += mask_grad
+            blocks_ref[slot, POOLED : POOLED + CH, :] += feat
+            blocks_ref[slot, POOLED + CH : GROWS, :] += bias_grad
+        total_ref[rows, :] += dot(mixed, mask, NT)
+
+    def back_copy(m):
+        peer = source_of(m)
+        return remote(bsend_ref.at[m], brecv_ref.at[m], back_s, back_r, m, m, {"sess": peer})
+
+    def send_back(m, carry):
+        bsend_ref[m] = total_ref[pl.ds(pl.multiple_of(m * CH, CH), CH), :].astype(BF16)
+
+        @pl.when(m > 0)
+        def _():
+            back_copy(m).start()
+
+        return carry
+
+    def first_pass(i, carry):
+        t, h = i // 2, i % 2
+        readout(h * 4 + t, t * 2 + jnp.where(h == 0, 1 - core, core), 0)
+        return carry
+
+    lax.fori_loop(1, HALF, wait_pooled, 0)
+    turned_ref[...] = precv_ref[0:HALF].reshape(HALF * CH, POOLED).T
+    lax.fori_loop(0, 8, first_pass, 0)
+    lax.fori_loop(0, HALF, send_back, 0)
+    brecv_ref[0] = bsend_ref[0]
+    lax.fori_loop(HALF, 16, wait_pooled, 0)
+    turned_ref[...] = precv_ref[HALF:16].reshape(HALF * CH, POOLED).T
+
+    def turn_of(i):
+        return (row_y + jnp.where(i == 0, 2, jnp.where(i == 1, 1, jnp.where(i == 2, 3, 0)))) % 4
+
+    def take_pair(t):
+        pair_copy(t).wait()
+        blocks_ref[4 + t] += got_ref[t]
 
     def phase(i, carry):
-        t = (row_y + jnp.where(i == 0, 2, jnp.where(i == 1, 1, jnp.where(i == 2, 3, 0)))) % 4
+        t = turn_of(i)
 
         def half(h, inner):
-            readout(h * 4 + t, t * 2 + jnp.where(h == 0, 1 - core, core))
+            readout(h * 4 + t, t * 2 + jnp.where(h == 0, 1 - core, core), 1)
 
             @pl.when(h == 0)
             def _():
@@ -359,24 +414,41 @@
             return inner
 
         lax.fori_loop(0, 2, half, 0)
-        pair_copy(t).wait()
-        blocks_ref[4 + t] += got_ref[t]
-
-        @pl.when(i == 0)
+
+        @pl.when(i > 0)
+        def _():
+            take_pair(turn_of(i - 1))
+
+        @pl.when(i == 1)
         def _():
             half_ref[0] = blocks_ref[at_two].astype(BF16)
             relay_low.start()
             relay_high.start()
 
-        @pl.when(i == 1)
+        @pl.when(i == 2)
         def _():
             half_ref[1, LOW:GROWS, :] = blocks_ref[at_one, LOW:GROWS, :].astype(BF16)
             right_high.start()
 
-        @pl.when(i == 2)
+        @pl.when(i == 3)
         def _():
             half_ref[1, 0:LOW, :] = blocks_ref[at_three, 0:LOW, :].astype(BF16)
             left_low.start()
+
+        return carry
+
+    lax.fori_loop(0, 4, phase, 0)
+    lax.fori_loop(HALF, 16, send_back, 0)
+
+    one_half = jnp.asarray(1.0, BF16)
+    zero_half = jnp.asarray(0.0, BF16)
+
+    def backward(i, carry):
+        steps = [i * GROUP + g for g in range(GROUP)]
+        clips = [target_of(m) for m in steps]
+
+        @pl.when(i == RELAY_AT)
+        def _():
             relay_low.wait()
             blocks_ref[at_one, 0:LOW, :] += low_ref[...].astype(F32)
             right_low.start()
@@ -384,41 +456,13 @@
             blocks_ref[at_three, LOW:GROWS, :] += up_ref[...].astype(F32)
             left_high.start()
 
-        return carry
-
-    lax.fori_loop(0, 4, phase, 0)
-
-    def back_copy(j):
-        peer = (sess + 1 + j) % 16
-        return remote(bsend_ref.at[peer], brecv_ref.at[sess], back_s, back_r, peer, sess, {"sess": peer})
-
-    def send_back(j, carry):
-        f = (sess + 1 + j) % 16
-        bsend_ref[f] = total_ref[pl.ds(pl.multiple_of(f * CH, CH), CH), :].astype(BF16)
-
-        @pl.when(j < 15)
-        def _():
-            back_copy(j).start()
-
-        return carry
-
-    lax.fori_loop(0, 16, send_back, 0)
-    brecv_ref[sess] = bsend_ref[sess]
-
-    one_half = jnp.asarray(1.0, BF16)
-    zero_half = jnp.asarray(0.0, BF16)
-
-    def backward(i, carry):
-        steps = [i * GROUP + g for g in range(GROUP)]
-        clips = [(sess + 16 - m) % 16 for m in steps]
-        for m, k in zip(steps, clips):
+        for m in steps:
 
             @pl.when(m > 0)
             def _():
-                there = (sess + m) % 16
-                remote(bsend_ref.at[there], brecv_ref.at[k], back_s, back_r, there, k, {"sess": there}).wait()
-
-        grads = [brecv_ref[k] * jnp.asarray(0.25, BF16) for k in clips]
+                back_copy(m).wait()
+
+        grads = [brecv_ref[m] * jnp.asarray(0.25, BF16) for m in steps]
         slopes = [one_half + jnp.minimum(feats_ref[k], zero_half) for k in clips]
         pre2_grad = [jnp.concatenate([g] * 4, axis=0) * s for g, s in zip(grads, slopes)]
         act1 = [act_ref[k] for k in clips]
@@ -434,20 +478,21 @@
     lax.fori_loop(0, 16 // GROUP, backward, 0)
 
     small = finish_small(gmix_ref, gconv_ref, gmixb_ref, fold_ref, loss_ref[...])
-    for piece in range(8):
-        ar_ref[piece] = small[piece * 8 : piece * 8 + 8]
+    for piece in range(16):
+        top, lane = piece // 2 * 8, piece % 2 * 128
+        ar_ref[piece] = small[top : top + 8, lane : lane + 128]
 
     def a1_copy(j, here):
+        peer = (sess + 1 + j) % 16
+        return remote(ar_ref.at[peer], r1_ref.at[here], a1_s, a1_r, peer, here, {"sess": peer})
+
+    def a2_copy(j, here):
         peer = (clip + 1 + j) % 8
-        return remote(ar_ref.at[peer], r1_ref.at[here], a1_s, a1_r, peer, here, {"clip": peer})
-
-    def a2_copy(j, here):
+        return remote(s2_ref, r2_ref.at[here], a2_s, a2_r, peer, here, {"clip": peer})
+
+    def a3_copy(j, here):
         peer = (sess + 1 + j) % 16
-        return remote(s2_ref, r2_ref.at[here], a2_s, a2_r, peer, here, {"sess": peer})
-
-    def a3_copy(j, here):
-        peer = (clip + 1 + j) % 8
-        return remote(s3_ref, r3_ref.at[here], a3_s, a3_r, peer, here, {"clip": peer})
+        return remote(s3_ref, r3_ref.at[here], a3_s, a3_r, peer, here, {"sess": peer})
 
     def begin_all(copy, count, mine):
         def begin(j, carry):
@@ -463,18 +508,19 @@
 
         lax.fori_loop(0, count, finish, 0)
 
-    begin_all(a1_copy, 7, clip)
-    r1_ref[clip] = ar_ref[clip]
-    finish_all(a1_copy, 7, clip)
+    begin_all(a1_copy, 15, sess)
+    r1_ref[sess] = ar_ref[sess]
+    finish_all(a1_copy, 15, sess)
     part = jnp.sum(r1_ref[...], axis=0)
     s2_ref[...] = part
-    begin_all(a2_copy, 15, sess)
-    r2_ref[sess] = part
-    finish_all(a2_copy, 15, sess)
+    begin_all(a2_copy, 7, clip)
+    r2_ref[clip] = part
+    finish_all(a2_copy, 7, clip)
     part = jnp.sum(r2_ref[...], axis=0)
     s3_ref[...] = part
-    begin_all(a3_copy, 7, clip)
-    r3_ref[clip] = part
+    begin_all(a3_copy, 15, sess)
+    r3_ref[sess] = part
+    take_pair(row_y)
     right_high.wait()
     left_low.wait()
     right_low.wait()
@@ -483,8 +529,9 @@
     grads_out[0:LOW, :] = low + plus_low_ref[...].astype(F32)
     top = blocks_ref[4 + row_y, LOW:GROWS, :] + plus_high_ref[...]
     grads_out[LOW:GROWS, :] = top + minus_high_ref[...].astype(F32)
-    finish_all(a3_copy, 7, clip)
-    small_out[...] = r3_ref[...].reshape(CH, 256)
+    finish_all(a3_copy, 15, sess)
+    lines = [jnp.concatenate([r3_ref[2 * r], r3_ref[2 * r + 1]], axis=1) for r in range(8)]
+    small_out[...] = jnp.concatenate(lines, axis=0)
 
 
 def split_kernel(
@@ -547,9 +594,9 @@
             vmem((16, 16, 256), BF16),
             vmem((16, 16, 256), BF16),
             vmem((256, 256), F32),
-            vmem((POOLED, 1024), BF16),
-            vmem((1024, NBLOCK), F32),
-            vmem((1024, NBLOCK), BF16),
+            vmem((POOLED, HALF * CH), BF16),
+            vmem((HALF * CH, NBLOCK), F32),
+            vmem((HALF * CH, NBLOCK), BF16),
             vmem((1024, POOLED), F32),
             vmem((1, 1), F32),
             vmem((8, GROWS, NBLOCK), F32),
@@ -566,14 +613,14 @@
             vmem((256, 256), F32),
             vmem((256, 256), F32),
             vmem((CH, POOLED), F32),
-            vmem((8, 8, 256), F32),
-            vmem((8, 8, 256), F32),
-            vmem((8, 256), F32),
-            vmem((16, 8, 256), F32),
-            vmem((8, 256), F32),
-            vmem((8, 8, 256), F32),
+            vmem((16, 8, 128), F32),
+            vmem((16, 8, 128), F32),
+            vmem((8, 128), F32),
+            vmem((8, 8, 128), F32),
+            vmem((8, 128), F32),
+            vmem((16, 8, 128), F32),
         ]
-        + [dma(n) for n in (2, 2, 2, 16, 16, 16, 16, 4, 4, 6, 6, 16, 16, 8, 8, 16, 16, 8, 8)],
+        + [dma(n) for n in (2, 2, 2, 16, 16, 16, 16, 4, 4, 6, 6, 16, 16, 16, 16, 8, 8, 16, 16)],
         compiler_params=pltpu.CompilerParams(
             collective_id=0, has_side_effects=True, vmem_limit_bytes=VM
         ),

time: 101 us -> 95.1 us (0.942)
  Pallas kernels: 99.9 us -> 93.6 us
    pallas_call x1, Pallas kernels: 97.4 us -> 91.1 us  [run_step(): pl.pallas_call(functools.partial(step_kernel, loss_scale), in_specs=[smem...]
where the time goes in v3:
time: 95.1 us; the launch traced here: 94.9 us
  Pallas kernels  93.6 us (98%)
  between operations  1.29 us (1%)
    pallas_call x1, Pallas kernels, run_step(): pl.pallas_call(functools.partial(step_kernel, loss_scale), in_specs=[smem...  91.1 us
    pallas_call x1, Pallas kernels, run_split(): pl.pallas_call(split_kernel, out_shape=[jax.ShapeDtypeStruct(shape, F32)...  2.51 us

profile of v3, /device:TPU:1, one launch (start us, length us, event | category | flops | bytes accessed | tf_op | source)
XLA Modules:
  0.0 94.9 jit_solution(14159557091794525162)
XLA Ops:
  1.3 91.1 %train_step.1 = (f32[64,256]{1,0:T(8,128)}, f32[656,512]{1,0:T(8,128)}) custom-call(s32[1]{0:T(128)S(6)} %copy.21.count_ref, bf16[16,2304]{1,0:T(8,128)(2,1)} %bitcast.19, bf16[16,4096]{1,0:T(8,128)(2,1)} %bitcast.18, s32[1,16]{1,0:T(1,128)} %bitcast.20, bf16[64,147]{1,0:T(8,128)(2,1)} %weight_ref.1, f32[1,64]{1,0:T(1,128)} %bitcast.21, ...), custom_call_target="tpu_custom_call" | custom-call | tf_op jit(solution)/shard_map/train_step/pallas_call | solution.py:574
  92.4 2.5 %split_results.1 = (f32[1,1]{1,0:T(1,128)}, f32[64,147]{1,0:T(8,128)}, f32[1,64]{1,0:T(1,128)}, f32[64,64]{1,0:T(8,128)}, f32[1,64]{1,0:T(1,128)}, /*index=5*/f3...) custom-call(f32[64,256]{1,0:T(8,128)} %get-tuple-element.18.small_ref, f32[656,512]{1,0:T(8,128)} %get-tuple-element.19.grads_ref), custom_call_target="tpu_custom_call" | custom-call | tf_op jit(solution)/shard_map/split_results/pallas_call | solution.py:555

commit v4 on v3

--- a/solution.py
+++ b/solution.py
@@ -170,7 +170,7 @@
     mask_ref, featw_ref, planes_ref, prev_ref, after_ref, base_ref, w2_ref, mix4_ref, mixt_ref,
     patches_ref, act_ref, feats_ref, psend_ref, precv_ref, tsend_ref, trecv_ref, target_ref,
     turned_ref, proj_ref, mixed_ref, total_ref, loss_ref,
-    blocks_ref, got_ref, half_ref, low_ref, up_ref, minus_low_ref, minus_high_ref, plus_low_ref, plus_high_ref, bsend_ref, brecv_ref,
+    blocks_ref, got_ref, half_ref, low_ref, up_ref, minus_low_ref, minus_high_ref, plus_low_ref, plus_high_ref, brecv_ref,
     gmix_ref, gconv_ref, gmixb_ref, ar_ref, r1_ref, s2_ref, r2_ref, s3_ref, r3_ref,
     local_sem, halo_s, halo_r, pool_s, pool_r, targ_s, targ_r, pair_s, pair_r, ring_s, ring_r,
     back_s, back_r, a1_s, a1_r, a2_s, a2_r, a3_s, a3_r,
@@ -212,27 +212,9 @@
 
     planes = split_planes(video_ref[...], table_ref[...])
     planes_ref[...] = jnp.concatenate(planes, axis=0).astype(BF16)
-    pl.semaphore_wait(barrier, 22)
-
-    halo_up = remote(planes_ref, prev_ref, halo_s, halo_r, 0, 0, {"sess": (sess + 1) % 16})
-    halo_down = remote(planes_ref, after_ref, halo_s, halo_r, 1, 1, {"sess": (sess + 15) % 16})
-    halo_up.start()
-    halo_down.start()
-
     sort = sorting_matrix(assign_ref[...])
     stacked = jnp.concatenate([responses_ref[:, q * 256 : (q + 1) * 256] for q in range(16)], axis=0)
     tsend_ref[...] = dot(sort, stacked).astype(BF16).reshape(16, 16, 256)
-
-    def target_copy(m):
-        peer = target_of(m)
-        return remote(tsend_ref.at[peer], trecv_ref.at[m], targ_s, targ_r, m, m, {"sess": peer})
-
-    def start_target(m, carry):
-        target_copy(m).start()
-        return carry
-
-    lax.fori_loop(1, 16, start_target, 0)
-    trecv_ref[0] = tsend_ref[sess]
 
     conv_matrix(weight_ref[...], fold_ref, w2_ref)
     mix = mix_ref[...].astype(F32)
@@ -241,6 +223,29 @@
     bias1 = column(bias1_ref[...])
     bias2 = column(bias2_ref[...])
     masks = column_masks()
+
+    total_ref[...] = jnp.zeros_like(total_ref)
+    loss_ref[...] = jnp.zeros_like(loss_ref)
+    gmix_ref[...] = jnp.zeros_like(gmix_ref)
+    gconv_ref[...] = jnp.zeros_like(gconv_ref)
+    gmixb_ref[...] = jnp.zeros_like(gmixb_ref)
+    pl.semaphore_wait(barrier, 22)
+
+    halo_up = remote(planes_ref, prev_ref, halo_s, halo_r, 0, 0, {"sess": (sess + 1) % 16})
+    halo_down = remote(planes_ref, after_ref, halo_s, halo_r, 1, 1, {"sess": (sess + 15) % 16})
+    halo_up.start()
+    halo_down.start()
+
+    def target_copy(m):
+        peer = target_of(m)
+        return remote(tsend_ref.at[peer], trecv_ref.at[m], targ_s, targ_r, m, m, {"sess": peer})
+
+    def start_target(m, carry):
+        target_copy(m).start()
+        return carry
+
+    lax.fori_loop(1, 16, start_target, 0)
+    trecv_ref[0] = tsend_ref[sess]
 
     halo_up.wait()
     halo_down.wait()
@@ -279,11 +284,6 @@
 
     lax.fori_loop(0, 16 // GROUP, forward, 0)
     precv_ref[0] = psend_ref[sess]
-    total_ref[...] = jnp.zeros_like(total_ref)
-    loss_ref[...] = jnp.zeros_like(loss_ref)
-    gmix_ref[...] = jnp.zeros_like(gmix_ref)
-    gconv_ref[...] = jnp.zeros_like(gconv_ref)
-    gmixb_ref[...] = jnp.zeros_like(gmixb_ref)
     mask_copy.wait()
     featw_copy.wait()
 
@@ -327,53 +327,60 @@
     right_low = ring_copy(lows(blocks_ref.at[at_one]), minus_low_ref, 4, right)
     left_high = ring_copy(highs(blocks_ref.at[at_three]), plus_high_ref, 5, left)
 
-    def readout(slot, n, half):
-        at = pl.ds(pl.multiple_of(n * NBLOCK, NBLOCK), NBLOCK)
+    def readout(t, half):
+        parts = (0, 1)
+        slots = [t, 4 + t]
+        blocks = [t * 2 + 1 - core, t * 2 + core]
+        spans = [pl.ds(pl.multiple_of(n * NBLOCK, NBLOCK), NBLOCK) for n in blocks]
         frames = slice(half * HALF, (half + 1) * HALF)
-        rows = slice(half * HALF * CH, (half + 1) * HALF * CH)
-        mask = mask_ref[:, at]
-        weight = featw_ref[:, at].astype(F32)
-        proj_ref[...] = dot(precv_ref[frames].reshape(HALF * CH, POOLED), mask)
-        drives = []
-        for f in range(HALF):
-            drives.append(jnp.sum(proj_ref[f * CH : (f + 1) * CH, :] * weight, axis=0, keepdims=True))
-        drive = jnp.concatenate(drives, axis=0) + rbias_ref[:, at]
-        first = target_ref[pl.ds(pl.multiple_of(n * 32 + half * HALF, HALF), HALF), :]
-        second = target_ref[pl.ds(pl.multiple_of(n * 32 + 16 + half * HALF, HALF), HALF), :]
-        target = jnp.concatenate([first, second], axis=1)
-        small = jnp.exp(-jnp.abs(drive))
-        rate = jnp.maximum(drive, 0.0) + jnp.log1p(small) + 0.1
-        sigmoid = jnp.where(drive >= 0, 1.0, small) / (1.0 + small)
-        place = n * NBLOCK + lax.broadcasted_iota(jnp.int32, (HALF, NBLOCK), 1)
-        alive = place < count_ref[0]
-        terms = jnp.where(alive, rate - target * jnp.log(rate), 0.0)
-        loss_ref[...] += jnp.sum(terms, keepdims=True) * loss_scale
-        grad_drive = jnp.where(alive, (1.0 - target / rate) * sigmoid, 0.0) * loss_scale
-        feat = jnp.zeros((CH, NBLOCK), F32)
-        for f in range(HALF):
-            line = grad_drive[f : f + 1, :]
-            feat += line * proj_ref[f * CH : (f + 1) * CH, :]
-            mixed_ref[f * CH : (f + 1) * CH, :] = (line * weight).astype(BF16)
-        bias_grad = jnp.sum(grad_drive, axis=0, keepdims=True)
-        bias_grad = jnp.broadcast_to(bias_grad, (GROWS - POOLED - CH, NBLOCK))
-        mixed = mixed_ref[...]
-        mask_grad = dot(turned_ref[...], mixed)
-        if half == 0:
-            blocks_ref[slot, 0:POOLED, :] = mask_grad
-            blocks_ref[slot, POOLED : POOLED + CH, :] = feat
-            blocks_ref[slot, POOLED + CH : GROWS, :] = bias_grad
-        else:
-            blocks_ref[slot, 0:POOLED, :] += mask_grad
-            blocks_ref[slot, POOLED : POOLED + CH, :] += feat
-            blocks_ref[slot, POOLED + CH : GROWS, :] += bias_grad
-        total_ref[rows, :] += dot(mixed, mask, NT)
+        pooled = precv_ref[frames].reshape(HALF * CH, POOLED)
+        for p in parts:
+            proj_ref[p] = dot(pooled, mask_ref[:, spans[p]])
+        grad_drives = []
+        for p in parts:
+            n = blocks[p]
+            weight = featw_ref[:, spans[p]].astype(F32)
+            drives = []
+            for f in range(HALF):
+                drives.append(jnp.sum(proj_ref[p, f * CH : (f + 1) * CH, :] * weight, axis=0, keepdims=True))
+            drive = jnp.concatenate(drives, axis=0) + rbias_ref[:, spans[p]]
+            first = target_ref[pl.ds(pl.multiple_of(n * 32 + half * HALF, HALF), HALF), :]
+            second = target_ref[pl.ds(pl.multiple_of(n * 32 + 16 + half * HALF, HALF), HALF), :]
+            target = jnp.concatenate([first, second], axis=1)
+            small = jnp.exp(-jnp.abs(drive))
+            rate = jnp.maximum(drive, 0.0) + jnp.log1p(small) + 0.1
+            sigmoid = jnp.where(drive >= 0, 1.0, small) / (1.0 + small)
+            place = n * NBLOCK + lax.broadcasted_iota(jnp.int32, (HALF, NBLOCK), 1)
+            alive = place < count_ref[0]
+            terms = jnp.where(alive, rate - target * jnp.log(rate), 0.0)
+            loss_ref[...] += jnp.sum(terms, keepdims=True) * loss_scale
+            grad_drives.append(jnp.where(alive, (1.0 - target / rate) * sigmoid, 0.0) * loss_scale)
+            for f in range(HALF):
+                mixed_ref[p, f * CH : (f + 1) * CH, :] = (grad_drives[p][f : f + 1, :] * weight).astype(BF16)
+        mask_grads = [dot(turned_ref[...], mixed_ref[p]) for p in parts]
+        total_ref[...] += sum(dot(mixed_ref[p], mask_ref[:, spans[p]], NT) for p in parts)
+        for p in parts:
+            slot = slots[p]
+            feat = jnp.zeros((CH, NBLOCK), F32)
+            for f in range(HALF):
+                feat += grad_drives[p][f : f + 1, :] * proj_ref[p, f * CH : (f + 1) * CH, :]
+            bias_grad = jnp.sum(grad_drives[p], axis=0, keepdims=True)
+            bias_grad = jnp.broadcast_to(bias_grad, (GROWS - POOLED - CH, NBLOCK))
+            if half == 0:
+                blocks_ref[slot, 0:POOLED, :] = mask_grads[p]
+                blocks_ref[slot, POOLED : POOLED + CH, :] = feat
+                blocks_ref[slot, POOLED + CH : GROWS, :] = bias_grad
+            else:
+                blocks_ref[slot, 0:POOLED, :] += mask_grads[p]
+                blocks_ref[slot, POOLED : POOLED + CH, :] += feat
+                blocks_ref[slot, POOLED + CH : GROWS, :] += bias_grad
 
     def back_copy(m):
         peer = source_of(m)
-        return remote(bsend_ref.at[m], brecv_ref.at[m], back_s, back_r, m, m, {"sess": peer})
+        return remote(psend_ref.at[m], brecv_ref.at[m], back_s, back_r, m, m, {"sess": peer})
 
     def send_back(m, carry):
-        bsend_ref[m] = total_ref[pl.ds(pl.multiple_of(m * CH, CH), CH), :].astype(BF16)
+        psend_ref[m] = total_ref[pl.ds(pl.multiple_of(m % HALF * CH, CH), CH), :].astype(BF16)
 
         @pl.when(m > 0)
         def _():
@@ -381,17 +388,17 @@
 
         return carry
 
-    def first_pass(i, carry):
-        t, h = i // 2, i % 2
-        readout(h * 4 + t, t * 2 + jnp.where(h == 0, 1 - core, core), 0)
+    def first_pass(t, carry):
+        readout(t, 0)
         return carry
 
     lax.fori_loop(1, HALF, wait_pooled, 0)
     turned_ref[...] = precv_ref[0:HALF].reshape(HALF * CH, POOLED).T
-    lax.fori_loop(0, 8, first_pass, 0)
+    lax.fori_loop(0, 4, first_pass, 0)
+    lax.fori_loop(HALF, 16, wait_pooled, 0)
     lax.fori_loop(0, HALF, send_back, 0)
-    brecv_ref[0] = bsend_ref[0]
-    lax.fori_loop(HALF, 16, wait_pooled, 0)
+    total_ref[...] = jnp.zeros_like(total_ref)
+    brecv_ref[0] = psend_ref[0]
     turned_ref[...] = precv_ref[HALF:16].reshape(HALF * CH, POOLED).T
 
     def turn_of(i):
@@ -403,17 +410,8 @@
 
     def phase(i, carry):
         t = turn_of(i)
-
-        def half(h, inner):
-            readout(h * 4 + t, t * 2 + jnp.where(h == 0, 1 - core, core), 1)
-
-            @pl.when(h == 0)
-            def _():
-                pair_copy(t).start()
-
-            return inner
-
-        lax.fori_loop(0, 2, half, 0)
+        readout(t, 1)
+        pair_copy(t).start()
 
         @pl.when(i > 0)
         def _():
@@ -595,9 +593,9 @@
             vmem((16, 16, 256), BF16),
             vmem((256, 256), F32),
             vmem((POOLED, HALF * CH), BF16),
-            vmem((HALF * CH, NBLOCK), F32),
-            vmem((HALF * CH, NBLOCK), BF16),
-            vmem((1024, POOLED), F32),
+            vmem((2, HALF * CH, NBLOCK), F32),
+            vmem((2, HALF * CH, NBLOCK), BF16),
+            vmem((HALF * CH, POOLED), F32),
             vmem((1, 1), F32),
             vmem((8, GROWS, NBLOCK), F32),
             vmem((4, GROWS, NBLOCK), F32),
@@ -608,7 +606,6 @@
             vmem((GROWS - LOW, NBLOCK), BF16),
             vmem((LOW, NBLOCK), BF16),
             vmem((GROWS - LOW, NBLOCK), F32),
-            vmem((16, CH, POOLED), BF16),
             vmem((16, CH, POOLED), BF16),
             vmem((256, 256), F32),
             vmem((256, 256), F32),

time: 95.1 us -> 93.5 us (0.983)
  Pallas kernels: 93.6 us -> 92 us
    pallas_call x1, Pallas kernels: 91.1 us -> 89.5 us  [run_step(): pl.pallas_call(functools.partial(step_kernel, loss_scale), in_specs=[smem...]
where the time goes in v4:
time: 93.5 us; the launch traced here: 93.3 us
  Pallas kernels  92 us (98%)
  between operations  1.29 us (1%)
    pallas_call x1, Pallas kernels, run_step(): pl.pallas_call(functools.partial(step_kernel, loss_scale), in_specs=[smem...  89.5 us
    pallas_call x1, Pallas kernels, run_split(): pl.pallas_call(split_kernel, out_shape=[jax.ShapeDtypeStruct(shape, F32)...  2.51 us

profile of v4, /device:TPU:1, one launch (start us, length us, event | category | flops | bytes accessed | tf_op | source)
XLA Modules:
  0.0 93.3 jit_solution(18232318021734210581)
XLA Ops:
  1.3 89.5 %train_step.1 = (f32[64,256]{1,0:T(8,128)}, f32[656,512]{1,0:T(8,128)}) custom-call(s32[1]{0:T(128)S(6)} %copy.21.count_ref, bf16[16,2304]{1,0:T(8,128)(2,1)} %bitcast.19, bf16[16,4096]{1,0:T(8,128)(2,1)} %bitcast.18, s32[1,16]{1,0:T(1,128)} %bitcast.20, bf16[64,147]{1,0:T(8,128)(2,1)} %weight_ref.1, f32[1,64]{1,0:T(1,128)} %bitcast.21, ...), custom_call_target="tpu_custom_call" | custom-call | tf_op jit(solution)/shard_map/train_step/pallas_call | solution.py:572
  90.8 2.5 %split_results.1 = (f32[1,1]{1,0:T(1,128)}, f32[64,147]{1,0:T(8,128)}, f32[1,64]{1,0:T(1,128)}, f32[64,64]{1,0:T(8,128)}, f32[1,64]{1,0:T(1,128)}, /*index=5*/f3...) custom-call(f32[64,256]{1,0:T(8,128)} %get-tuple-element.18.small_ref, f32[656,512]{1,0:T(8,128)} %get-tuple-element.19.grads_ref), custom_call_target="tpu_custom_call" | custom-call | tf_op jit(solution)/shard_map/split_results/pallas_call | solution.py:553
